TPU v7x, 32 devices: a whole 2x2x4 slice. The times are simulated.
32 devices in a mesh: row: 4 (over y, x), col: 4 (over z), depth: 2 (over core).
Axes of the slice: x: 2, y: 2, z: 4, core: 2. Of those that a mesh axis runs over, the one named last changes fastest.
Arguments:
- covariance: float32 [12, 4, 12, 4, 256, 256], P(None, 'row', None, 'col'), may hold values from 0 to 2, as said below
Outputs:
- factored: float32 [12, 4, 12, 4, 256, 256], P(None, 'row', None, 'col', 'depth')
Inputs may be any that keep to these rules, and one draw needn't show every extreme that they name: covariance is the Matern kernel of smoothness 3/2, (1 + rho) exp(-rho) with rho = sqrt(3) times the scaled distance, over 12288 points in the unit cube of 8 coordinates with length scales between 0.3 and 1.2, plus a nugget between 0.2 and 1 on the diagonal; it is symmetric positive definite.
All inputs are finite; a program needn't handle non-finite values.
Results may differ from a plain program's by a relative error of at most 0.0003.
Values sent between devices are 32-bit elements; how exact they have to be, the bound alone decides.
No kernel may reach another device: no remote copies, remote signals or barrier semaphores. Data moves between devices by JAX's collectives and lax.ppermute only.
A program may use at most 192 MiB of HBM per device.

v0:
```python
import jax
import jax.numpy as jnp
from jax import lax
from jax.sharding import PartitionSpec as P

ORDER = 12288
TILE = 256
STEPS = 1


EXACT = lax.Precision.HIGHEST


def spread(value, axis, source):
    kept = jnp.where(lax.axis_index(axis) == source, value, 0).astype(value.dtype)
    return lax.psum(kept, axis)


def factor_panel(column_tiles, panel_step, row_global):
    panel_width = 2 * TILE
    column_parts = [
        spread(column_tiles, "col", 2 * panel_step + column_side) for column_side in range(2)
    ]
    panel_rows = jnp.concatenate(column_parts, axis=2)
    block_parts = [spread(panel_rows[0], "row", 2 * panel_step + row_side) for row_side in range(2)]
    diagonal_block = jnp.concatenate(block_parts, axis=0)
    factor_lower = jnp.linalg.cholesky(diagonal_block)
    identity = jnp.eye(panel_width, dtype=jnp.float32)
    inverse_lower = jax.scipy.linalg.solve_triangular(factor_lower, identity, lower=True)
    flattened = panel_rows.reshape(-1, panel_width)
    solved = jnp.dot(flattened, inverse_lower.T, precision=EXACT)
    solved = solved.reshape(panel_rows.shape)
    keep_rows = (row_global >= panel_step * panel_width)[:, :, None]
    return jnp.where(keep_rows, solved, 0.0)


def on_device(covariance):
    rows_count = lax.axis_size("row")
    cols_count = lax.axis_size("col")
    row_index = lax.axis_index("row")
    col_index = lax.axis_index("col")
    depth_index = lax.axis_index("depth")
    tiles_side = ORDER // TILE
    tile_rows = tiles_side // rows_count
    tile_cols = tiles_side // cols_count
    per_column = rows_count // cols_count
    half_tile = TILE // 2
    panel_width = 2 * TILE
    factored_width = STEPS * panel_width
    tile_offsets = jnp.arange(TILE, dtype=jnp.int32)
    row_global = (
        jnp.arange(tile_rows, dtype=jnp.int32)[:, None] * rows_count + row_index
    ) * TILE + tile_offsets[None, :]
    col_global = (
        jnp.arange(tile_cols, dtype=jnp.int32)[:, None] * cols_count + col_index
    ) * TILE + tile_offsets[None, :]
    local_tiles = covariance.reshape(tile_rows, tile_cols, TILE, TILE)
    held_ids = lax.dynamic_slice_in_dim(row_global, depth_index * half_tile, half_tile, 1)
    held_tiles = lax.dynamic_slice_in_dim(local_tiles, depth_index * half_tile, half_tile, 2)
    partial_value = held_tiles
    column_tiles = lax.all_gather(partial_value[:, 0], "depth", axis=1, tiled=True)
    factor = factor_panel(column_tiles, 0, row_global)
    received = [
        spread(factor, "row", col_index + copy_index * cols_count)
        for copy_index in range(per_column)
    ]
    col_factor = jnp.stack(received, 1).reshape(tile_cols, TILE, panel_width)
    own_half = lax.dynamic_slice_in_dim(factor, depth_index * half_tile, half_tile, 1)
    partial_value = partial_value - jnp.einsum(
        "aik,bjk->abij", own_half, col_factor, precision=EXACT
    )
    tile_start = jnp.minimum(col_index, 2 * STEPS - 1) * TILE
    factor_tile = lax.dynamic_slice_in_dim(factor, tile_start, TILE, 2)
    factor_tile = lax.dynamic_slice_in_dim(factor_tile, depth_index * half_tile, half_tile, 1)
    first_column = jnp.where(col_index < 2 * STEPS, factor_tile, partial_value[:, 0])
    partial_value = partial_value.at[:, 0].set(first_column)
    upper_part = (held_ids < factored_width)[:, None, :, None] & (col_global >= factored_width)[
        None, :, None, :
    ]
    partial_value = jnp.where(upper_part, 0.0, partial_value)
    return partial_value.reshape(tile_rows, 1, tile_cols, 1, half_tile, TILE)


def solution(mesh):
    in_specs = (P(None, "row", None, "col", None, None),)
    out_specs = P(None, "row", None, "col", "depth", None)
    return jax.shard_map(
        on_device, mesh=mesh, in_specs=in_specs, out_specs=out_specs, check_vma=False
    )
```

profile of v0, /device:TPU:0, one launch (start us, length us, event | category | flops | bytes accessed | tf_op | source)
XLA Modules:
  0.0 713.6 jit_solution(18278233365104775281)
XLA Ops:
  6.5 12.9 %constant_dynamic-slice_fusion.1 = f32[12,1,12,1,128,256]{5,4,3,2,1,0:T(8,128)} fusion(f32[12,1,12,1,256,256]{5,4,3,2,1,0:T(8,128)} %param.3, s32[]{:T(128)S(6)} %select_n.75), kind=kLoop, calls=%fused_computation.92 | loop fusion | bytes 37748740 | tf_op jit(solution)/shard_map/dynamic_slice | solution.py:59
  19.4 18.7 %copy.2 = f32[12,1,12,1,128,256]{4,5,0,2,3,1:T(8,128)} copy(f32[12,1,12,1,128,256]{5,4,3,2,1,0:T(8,128)} %constant_dynamic-slice_fusion.1) | data formatting | bytes 37748736 | tf_op jit(solution)/shard_map/dynamic_slice | solution.py:59
  38.1 2.7 slice.163
  40.8 14.4 %all-gather.3.cloned.1.call-done = f32[12,1,256,256]{2,3,0,1:T(8,128)} async-done(((f32[12,1,128,256]{2,3,0,1:T(8,128)}), f32[12,1,256,256]{2,3,0,1:T(8,128)}) %all-gather.3.cloned.1.call-update) | async-done | bytes 3145744 | tf_op jit(solution)/shard_map/all_gather | solution.py:61
  55.3 5.3 select_bitcast_fusion.1
  60.6 224.5 %all-reduce.9.cloned.1.call-done = (f32[12,256,256]{1,2,0:T(8,128)}, f32[12,256,256]{1,2,0:T(8,128)}) async-done(((f32[12,256,256]{1,2,0:T(8,128)}, f32[12,256,256]{1,2,0:T(8,128)}), (f32[12,256,256]{1,2,0:T(8,128)}, f32[12,256,256]{1,2,0:T(8,128)})) %all-reduce.9.cloned.1.call-update) | async-done | bytes 6291472 | tf_op jit(solution)/shard_map/psum | solution.py:16
  285.2 2.4 constant_dynamic-update-slice_fusion.1
  288.3 2.7 copy-done
  291.0 1.1 select_bitcast_fusion.3
  292.4 51.5 %all-reduce.11.cloned.1.call-done = (f32[256,512]{0,1:T(8,128)}, f32[256,512]{0,1:T(8,128)}) async-done(((f32[256,512]{0,1:T(8,128)}, f32[256,512]{0,1:T(8,128)}), (f32[256,512]{0,1:T(8,128)}, f32[256,512]{0,1:T(8,128)})) %all-reduce.11.cloned.1.call-update) | async-done | bytes 1048592 | tf_op jit(solution)/shard_map/psum | solution.py:16
  343.9 1.1 constant_dynamic-update-slice_fusion.3
  345.0 1.1 constant_dynamic-update-slice_fusion.2
  346.7 1.0 copy-done.2
  347.7 11.7 %cholesky.104 = f32[128,128]{1,0:T(8,128)S(1)} custom-call(f32[128,128]{1,0:T(8,128)S(1)} %cholesky.266), custom_call_target="Cholesky" | custom-call | tf_op jit(solution)/shard_map/jit(cholesky)/cholesky | solution.py:27
  359.6 9.8 %custom-call.31 = f32[1,128,128]{1,2,0:T(8,128)S(1)} custom-call(f32[1,128,128]{2,1,0:T(8,128)S(1)} %get-tuple-element.52), custom_call_target="InvertDiagBlocksLowerTriangular" | custom-call | tf_op jit(solution)/shard_map/jit(cholesky)/cholesky | solution.py:27
  369.4 1.2 constant_dynamic-update-slice_fusion.4
  370.6 1.3 convolution_subtract_fusion.3
  371.9 11.7 %cholesky.217 = f32[128,128]{1,0:T(8,128)S(1)} custom-call(f32[128,128]{1,0:T(8,128)S(1)} %cholesky.270), custom_call_target="Cholesky" | custom-call | tf_op jit(solution)/shard_map/jit(cholesky)/cholesky | solution.py:27
  383.6 10.1 %custom-call.32 = f32[1,128,128]{1,2,0:T(8,128)S(1)} custom-call(f32[1,128,128]{2,1,0:T(8,128)S(1)} %get-tuple-element.49), custom_call_target="InvertDiagBlocksLowerTriangular" | custom-call | tf_op jit(solution)/shard_map/jit(cholesky)/cholesky | solution.py:27
  394.0 1.3 convolution_subtract_fusion.4
  395.4 11.7 %cholesky.238 = f32[128,128]{1,0:T(8,128)S(1)} custom-call(f32[128,128]{1,0:T(8,128)S(1)} %cholesky.275), custom_call_target="Cholesky" | custom-call | tf_op jit(solution)/shard_map/jit(cholesky)/cholesky | solution.py:27
  407.1 0.7 compare_reduce_fusion.1
  407.8 9.8 %custom-call.33 = f32[1,128,128]{1,2,0:T(8,128)S(1)} custom-call(f32[1,128,128]{2,1,0:T(8,128)S(1)} %get-tuple-element.46), custom_call_target="InvertDiagBlocksLowerTriangular" | custom-call | tf_op jit(solution)/shard_map/jit(cholesky)/cholesky | solution.py:27
  417.8 1.2 convolution_subtract_fusion.5
  419.0 11.9 %cholesky.255 = f32[128,128]{1,0:T(8,128)S(1)} custom-call(f32[128,128]{1,0:T(8,128)S(1)} %convolution_subtract_fusion.5), custom_call_target="Cholesky" | custom-call | tf_op jit(solution)/shard_map/jit(cholesky)/cholesky | solution.py:27
  430.9 0.6 compare_reduce_fusion
  431.5 0.7 compare_reduce_fusion.2
  434.8 10.3 %while.2 = (s32[]{:T(128)}, f32[512,512]{1,0:T(8,128)S(1)}, s32[4,2]{0,1:T(2,128)S(1)}, f32[4,128,128]{2,1,0:T(8,128)}, s32[]{:T(128)}) while((s32[]{:T(128)}, f32[512,512]{1,0:T(8,128)S(1)}, s32[4,2]{0,1:T(2,128)S(1)}, f32[4,128,128]{2,1,0:T(8,128)}, s32[]{:T(128)}) %tuple.34), condition=%wide.while_cond.1, body=%wide.while_body.1.sunk | while | flops 2 | bytes 132705 | solution.py:29
  434.9 0.6 fusion.53
  435.5 2.0 bitcast_dynamic-update-slice_fusion.2
  437.5 0.6 fusion.53
  438.0 1.9 bitcast_dynamic-update-slice_fusion.2
  440.0 0.6 fusion.53
  440.6 1.9 bitcast_dynamic-update-slice_fusion.2
  442.6 0.6 fusion.53
  443.1 1.9 bitcast_dynamic-update-slice_fusion.2
  445.1 40.1 %custom-call.34 = f32[4,128,128]{1,2,0:T(8,128)S(1)} custom-call(f32[4,128,128]{2,1,0:T(8,128)} %get-tuple-element.24), custom_call_target="InvertDiagBlocksLowerTriangular" | custom-call | tf_op jit(solution)/shard_map/jit(_solve_triangular)/triangular_solve | solution.py:29
  485.9 0.4 fusion.35
  486.3 0.4 convolution_subtract_fusion
  486.8 0.4 fusion.33
  487.2 0.6 convolution_subtract_fusion.2
  487.8 0.4 fusion.32
  488.3 15.5 %broadcast_select_fusion = (f32[12,256,512]{1,2,0:T(8,128)}, f32[12,256,512]{1,2,0:T(8,128)}) fusion(pred[]{:T(512)S(6)} %eq.24, f32[12,256,512]{1,2,0:T(8,128)} %copy-done, f32[128,512]{1,0:T(8,128)S(1)} %fusion.32, f32[128,512]{1,0:T(8,128)S(1)} %fusion.33, f32[128,512]{1,0:T(8,128)S(1)} %fusion.35, f32[128,512]{1,0:T(8,128)S(1)} %fusion.23, ...), kind=kOutput, calls=%fused_computation.9 | convolution fusion | flops 9667608576 | bytes 19926016 | tf_op jit(solution)/shard_map/dot_general | solution.py:31
  504.0 138.4 %all-reduce.7.cloned.1.call-done = f32[12,256,512]{1,2,0:T(8,128)} async-done(((f32[12,256,512]{1,2,0:T(8,128)}), f32[12,256,512]{1,2,0:T(8,128)}) %all-reduce.7.cloned.1.call-update) | async-done | bytes 6291472 | tf_op jit(solution)/shard_map/psum | solution.py:16
  642.5 34.6 %bitcast_subtract_fusion = f32[12,12,128,256]{2,3,0,1:T(8,128)S(1)} fusion(f32[12,256,512]{1,2,0:T(8,128)} %all-reduce.7.cloned.1.call-done, f32[12,256,512]{1,2,0:T(8,128)} %get-tuple-element.56, s32[]{:T(128)S(6)} %select_n.75, f32[12,1,12,1,128,256]{4,5,0,2,3,1:T(8,128)} %copy.2), kind=kOutput, calls=%fused_computation.2 | convolution fusion | flops 28995747840 | bytes 47185924 | tf_op jit(solution)/shard_map/aik,bjk->abij/dot_general | solution.py:69
  677.1 3.0 fusion.5
  680.1 8.1 %select_bitcast_fusion = f32[12,1,12,1,128,256]{4,5,0,2,3,1:T(8,128)} fusion(f32[12,12,128,256]{2,3,0,1:T(8,128)S(1)} %fusion.5, pred[12,256]{1,0:T(8,128)(4,1)S(1)} %add_compare_fusion, pred[12,128]{1,0:T(8,128)(4,1)S(1)} %dynamic-slice_compare_fusion), kind=kLoop, calls=%fused_computation.3 | loop fusion | flops 9437184 | bytes 37753344 | tf_op jit(solution)/shard_map/reshape | solution.py:81
  688.2 18.7 %copy.8 = f32[12,1,12,1,128,256]{5,4,3,2,1,0:T(8,128)} copy(f32[12,1,12,1,128,256]{4,5,0,2,3,1:T(8,128)} %select_bitcast_fusion) | data formatting | bytes 37748736 | tf_op jit(solution)/shard_map/reshape | solution.py:81
  (43 shorter events, 3.7 us)
Async XLA Ops:
  6.5 48.7 %all-gather.3.cloned.1.call-start = ((), (), s32[]{:S(2)}) async-start(), calls=%async_computation.1 | async-start | bytes 4718592 | tf_op jit(solution)/shard_map/all_gather | solution.py:61
  40.8 244.4 %all-reduce.9.cloned.1.call-start = ((), (), s32[]{:S(2)}) async-start(), calls=%async_computation.2 | async-start | bytes 12582912 | tf_op jit(solution)/shard_map/psum | solution.py:16
  60.6 283.3 %all-reduce.11.cloned.1.call-start = ((), (), s32[]{:S(2)}) async-start(), calls=%async_computation.3 | async-start | bytes 2097152 | tf_op jit(solution)/shard_map/psum | solution.py:16
  285.2 2.8 copy-start.1
  288.2 2.7 copy-start
  292.0 350.4 %all-reduce.7.cloned.1.call-start = ((), (), s32[]{:S(2)}) async-start(), calls=%async_computation | async-start | bytes 12582912 | tf_op jit(solution)/shard_map/psum | solution.py:16
  346.7 1.0 copy-start.2
Sparse Core Ops, SparseCore 0:
  40.9 14.3 all-gather.2
  60.7 224.4 all-reduce.8
  292.2 51.6 all-reduce.10
  504.0 138.4 all-reduce.6
where the time goes:
time: 724 us; the launch traced here: 714 us
  waiting for transfers between devices  429 us (59%)
  other arithmetic  137 us (19%)
  local copies, waits for them, and re-layouts  72.6 us (10%)
  matrix products  58.6 us (8%)
  between operations  16.1 us (2%)
    psum x3, waiting for transfers between devices, spread(): return lax.psum(kept, axis)  414 us
    another operation x14, other arithmetic, factor_panel(): factor_lower = jnp.linalg.cholesky(diagonal_block)  78.9 us
    another operation x3, other arithmetic, factor_panel(): jax.scipy.linalg.solve_triangular(factor_lower, identity, lower=True)  40.3 us
    dot_general x1, matrix products, on_device(): jnp.einsum('aik,bjk->abij', own_half, col_factor, precision=EXACT)  34.6 us
    dynamic_slice x2, local copies, waits for them, and re-layouts, on_device(): lax.dynamic_slice_in_dim(local_tiles, depth_index * half_tile, half_tile, 2)  31.6 us
    reshape x1, local copies, waits for them, and re-layouts, on_device(): return partial_value.reshape(tile_rows, 1, tile_cols, 1, half_tile, TILE)  18.7 us
    dot_general x1, matrix products, factor_panel(): solved = jnp.dot(flattened, inverse_lower.T, precision=EXACT)  15.5 us
  transfers between devices with their start and end apart: 4, of which 4 were waited for; matrix products, arithmetic and copies ran while one was open for 0% of the time, Pallas kernels for 0%

commit v1 on v0

v1 whole, which is shorter than its diff:
```python
import functools

import jax
import jax.numpy as jnp
from jax import lax
from jax.experimental import pallas as pl
from jax.experimental.pallas import tpu as pltpu
from jax.sharding import PartitionSpec as P

EXACT = lax.Precision.HIGHEST
F32 = jnp.float32
BF16 = jnp.bfloat16
LIMIT = 56 << 20
ANY = pl.BlockSpec(memory_space=pl.ANY)
LIGHT = pl.CostEstimate(flops=1, bytes_accessed=1, transcendentals=0)


def dot(a, b, ca=1, cb=0, precision=None):
    return lax.dot_general(
        a, b, (((ca,), (cb,)), ((), ())), precision=precision, preferred_element_type=F32
    )


def split(value):
    high = value.astype(BF16)
    return high, (value - high.astype(F32)).astype(BF16)


def diag_inverse(block, n, group=8):
    row_ids = lax.broadcasted_iota(jnp.int32, (n, n), 0)
    col_ids = lax.broadcasted_iota(jnp.int32, (n, n), 1)
    unit = jnp.where(row_ids == col_ids, 1.0, 0.0).astype(F32)
    sub = lax.broadcasted_iota(jnp.int32, (group, n), 0)
    count = n // group
    rows = [block[group * g : group * (g + 1)] for g in range(count)]
    inverse = [unit[group * g : group * (g + 1)] for g in range(count)]

    def lanes(value, index):
        return jnp.broadcast_to(value[:, index : index + 1], (group, n))

    def subs(value, index):
        return jnp.broadcast_to(value[index : index + 1], (group, n))

    done = []
    for g in range(count):
        first = group * g
        here, inv_here = rows[g], inverse[g]
        cols = [lanes(here, first + j) for j in range(group)]
        recips, pivots, inv_pivots, cross = [], [], [], {}
        scale = jnp.zeros((group, n), F32)
        for j in range(group):
            root = lax.rsqrt(subs(cols[j], j))
            recip = root * root
            scale = jnp.where(sub == j, root, scale)
            pivot, inv_pivot = subs(here, j), subs(inv_here, j)
            factor = jnp.where(sub > j, cols[j] * recip, 0.0)
            for later in range(j + 1, group):
                cross[j, later] = subs(cols[later], j)
                cols[later] = cols[later] - factor * cross[j, later]
            here = here - factor * pivot
            inv_here = inv_here - factor * inv_pivot
            recips.append(recip)
            pivots.append(pivot)
            inv_pivots.append(inv_pivot)
        done.append(inv_here * scale)
        for below in range(g + 1, count):
            value, inv_value = rows[below], inverse[below]
            cols = [lanes(value, first + j) for j in range(group)]
            for j in range(group):
                factor = cols[j] * recips[j]
                for later in range(j + 1, group):
                    cols[later] = cols[later] - factor * cross[j, later]
                value = value - factor * pivots[j]
                inv_value = inv_value - factor * inv_pivots[j]
            rows[below], inverse[below] = value, inv_value
    return jnp.concatenate(done, 0)


def factor_steps(matrix, out, start, stop, step):
    n = matrix.shape[0]
    for a in range(start, stop, step):
        e = a + step
        inv = diag_inverse(matrix[a:e, a:e], step)
        if a:
            out[a:e, :a] = dot(inv, out[a:e, :a], precision=EXACT)
        out[a:e, a:e] = inv
        if e < n:
            panel = dot(inv, matrix[a:e, e:], precision=EXACT)
            matrix[e:, e:] = matrix[e:, e:] - dot(panel, panel, 0, 0, EXACT)
            out[e:, :e] = out[e:, :e] - dot(panel, out[a:e, :e], 0, 0, EXACT)


def assemble_kernel(place, mine, across, mine_other, across_other, matrix, out, *, step):
    half = mine.shape[1]
    tile = mine.shape[2]
    parity = lax.rem(place[0], 2)
    depth = place[2]
    for ref, tile_row, side in (
        (mine, parity, depth),
        (across, 1 - parity, depth),
        (mine_other, parity, 1 - depth),
        (across_other, 1 - parity, 1 - depth),
    ):
        start = pl.multiple_of(tile_row * tile + side * half, half)
        for q in range(2):
            matrix[pl.ds(start, half), q * tile : (q + 1) * tile] = ref[q]
    out[...] = jnp.zeros_like(out)
    factor_steps(matrix, out, 0, step, step)


def eliminate_kernel(matrix_in, inv_in, matrix, inv, *, start, stop, step):
    matrix[...] = matrix_in[...]
    inv[...] = inv_in[...]
    factor_steps(matrix, inv, start, stop, step)


def factor_start(place, pieces, step):
    n = 2 * pieces[0].shape[-1]
    whole = pl.BlockSpec(memory_space=pltpu.VMEM)
    square = jax.ShapeDtypeStruct((n, n), F32)
    return pl.pallas_call(
        functools.partial(assemble_kernel, step=step),
        out_shape=[square, square],
        in_specs=[pl.BlockSpec(memory_space=pltpu.SMEM)] + [whole] * 4,
        out_specs=[whole] * 2,
        compiler_params=pltpu.CompilerParams(vmem_limit_bytes=16 << 20),
        cost_estimate=LIGHT,
        name="factor_start",
    )(place, *pieces)


def factor_next(matrix, inv, start, stop, step):
    n = matrix.shape[0]
    whole = pl.BlockSpec(memory_space=pltpu.VMEM)
    square = jax.ShapeDtypeStruct((n, n), F32)
    return pl.pallas_call(
        functools.partial(eliminate_kernel, start=start, stop=stop, step=step),
        out_shape=[square, square],
        in_specs=[whole] * 2,
        out_specs=[whole] * 2,
        compiler_params=pltpu.CompilerParams(vmem_limit_bytes=16 << 20),
        cost_estimate=LIGHT,
        name="factor_next",
    )(matrix, inv)


def columns_kernel(place, inv, *refs, parts):
    both_parts, first, raw = refs[-3:]
    group, half, tile = refs[0].shape
    n = 2 * tile
    parity = lax.rem(place[0], 2)
    depth = place[2]
    turn = pl.program_id(0) // (pl.num_programs(0) // parts)
    sides = ((parity, depth), (1 - parity, depth), (parity, 1 - depth), (1 - parity, 1 - depth))

    for part in range(parts):

        @pl.when(turn == part)
        def _(part=part):
            for ref, (q, side) in zip(refs[4 * part : 4 * part + 4], sides):
                start = pl.multiple_of(q * tile + side * half, half)
                for b in range(group):
                    raw[pl.ds(start, half), b * tile : (b + 1) * tile] = ref[b]

    for b in range(group):
        here = slice(b * tile, (b + 1) * tile)
        for start, stop in ((0, tile), (tile, n)):
            total = dot(inv[start:stop, :stop], raw[:stop, here], precision=EXACT)
            if start == 0:
                first[:, here] = jnp.broadcast_to(total[:1], (8, tile))
                total = jnp.where(lax.broadcasted_iota(jnp.int32, total.shape, 0) == 0, 0.0, total)
            high, low = split(total)
            both_parts[start:stop, here] = high
            both_parts[n + start : n + stop, here] = low


def columns(place, inv, pieces, parts, group):
    count, half, tile = pieces[0].shape
    n = 2 * tile
    steps = count // group
    width = group * tile

    def piece(part):
        return pl.BlockSpec(
            (group, half, tile), lambda j, place: (jnp.clip(j - part * steps, 0, steps - 1), 0, 0)
        )

    return pl.pallas_call(
        functools.partial(columns_kernel, parts=parts),
        out_shape=[
            jax.ShapeDtypeStruct((2 * n, parts * count * tile), BF16),
            jax.ShapeDtypeStruct((8, parts * count * tile), F32),
        ],
        grid_spec=pltpu.PrefetchScalarGridSpec(
            num_scalar_prefetch=1,
            grid=(parts * steps,),
            in_specs=[pl.BlockSpec((n, n), lambda j, place: (0, 0))]
            + [piece(number // 4) for number in range(len(pieces))],
            out_specs=[
                pl.BlockSpec((2 * n, width), lambda j, place: (0, j)),
                pl.BlockSpec((8, width), lambda j, place: (0, j)),
            ],
            scratch_shapes=[pltpu.VMEM((n, width), F32)],
        ),
        compiler_params=pltpu.CompilerParams(vmem_limit_bytes=LIMIT),
        cost_estimate=LIGHT,
        name="columns",
    )(place, inv, *pieces)


def update_kernel(place, inv, *refs, sources, plan, first_tile):
    cands = refs[:sources]
    top, top_first, tiles = refs[sources : sources + 3]
    out, raw, exact, lead, high, low = refs[-6:]
    chunk_rows, _, group, _, half, tile = out.shape
    n = 2 * tile
    step = pl.program_id(0)
    row, col = place[0], place[1]

    @pl.when(step == 0)
    def _():
        for number, offset, at_first, at_second, begin, size in plan:
            ref = cands[number]
            place_rows = slice(begin * half, (begin + size) * half)
            for at, lanes in ((at_first, slice(0, tile)), (at_second, slice(tile, n))):
                here = functools.reduce(jnp.logical_or, [col == index for index in at])

                @pl.when(here)
                def _(ref=ref, lanes=lanes, place_rows=place_rows, offset=offset, size=size):
                    raw[place_rows, lanes] = ref[offset : offset + size].reshape(size * half, tile)

        for start, stop in ((0, tile), (tile, n)):
            total = dot(raw[:, :stop], inv[start:stop, :stop], 1, 1, EXACT)
            exact[:, start:stop] = total
            if start == 0:
                lead[...] = jnp.broadcast_to(total[:, :1], lead.shape)
            high[:, start:stop], low[:, start:stop] = split(total)

    leads = jnp.concatenate([lead[...]] * (tile // 128), 1)
    for b in range(group):
        here = slice(b * tile, (b + 1) * tile)
        total = dot(high[...], top[:n, here])
        total += dot(high[...], top[n:, here])
        total += dot(low[...], top[:n, here])
        total += leads * top_first[:1, here]
        for a in range(chunk_rows):
            out[a, 0, b, 0] = tiles[a, 0, b, 0] - total[a * half : (a + 1) * half]

    @pl.when(jnp.logical_and(first_tile == 0, row < 2))
    def _():
        out[0] = jnp.zeros(out.shape[1:], F32)

    @pl.when(jnp.logical_and(step == 0, col < 2))
    def _():
        start = pl.multiple_of(jnp.minimum(col, 1) * tile, tile)
        panel = exact[:, pl.ds(start, tile)]
        for a in range(chunk_rows):
            out[a, 0, 0, 0] = panel[a * half : (a + 1) * half]


def update(place, inv, groups, top, covariance, before, first_tile, group):
    tile_rows, _, tile_cols, _, tile, _ = covariance.shape
    half = tile // 2
    n = 2 * tile
    cands, plan = [], []
    begin = 0
    for size, parts in groups:
        for array, offset, at_first, at_second in parts:
            number = next((i for i, known in enumerate(cands) if known is array), len(cands))
            if number == len(cands):
                cands.append(array)
            plan.append((number, offset, at_first, at_second, begin, size))
        begin += size
    chunk_rows = begin
    rows = chunk_rows * half
    width = group * tile
    chunk = first_tile // chunk_rows
    in_specs = [pl.BlockSpec((n, n), lambda j, place: (0, 0))]
    in_specs += [pl.BlockSpec(array.shape, lambda j, place: (0, 0, 0)) for array in cands]
    in_specs += [
        pl.BlockSpec((2 * n, width), lambda j, place: (0, j)),
        pl.BlockSpec((8, width), lambda j, place: (0, j)),
        pl.BlockSpec(
            (chunk_rows, 1, group, 1, half, tile),
            lambda j, place: (chunk, 0, j, 0, place[2], 0),
        ),
    ]
    operands = [place, inv, *cands, *top, covariance]
    aliases = {}
    if before is not None:
        in_specs.append(ANY)
        aliases = {len(operands): 0}
        operands.append(before)
    return pl.pallas_call(
        functools.partial(update_kernel, sources=len(cands), plan=plan, first_tile=first_tile),
        out_shape=jax.ShapeDtypeStruct((tile_rows, 1, tile_cols, 1, half, tile), F32),
        grid_spec=pltpu.PrefetchScalarGridSpec(
            num_scalar_prefetch=1,
            grid=(tile_cols // group,),
            in_specs=in_specs,
            out_specs=pl.BlockSpec(
                (chunk_rows, 1, group, 1, half, tile), lambda j, place: (chunk, 0, j, 0, 0, 0)
            ),
            scratch_shapes=[
                pltpu.VMEM((rows, n), F32),
                pltpu.VMEM((rows, n), F32),
                pltpu.VMEM((rows, 128), F32),
                pltpu.VMEM((rows, n), BF16),
                pltpu.VMEM((rows, n), BF16),
            ],
        ),
        input_output_aliases=aliases,
        compiler_params=pltpu.CompilerParams(vmem_limit_bytes=LIMIT),
        cost_estimate=pl.CostEstimate(
            flops=12 * rows * n * tile_cols * tile,
            bytes_accessed=8 * rows * tile_cols * tile,
            transcendentals=0,
        ),
        name="update",
    )(*operands)


def after(value, *earlier):
    return lax.optimization_barrier((value, *earlier))[0] if earlier else value


def outward(value, axis, turn=0):
    return lax.ppermute(value, axis, [(0, 3), (1, 2)] if turn else [(0, 2), (1, 3)])


def exchange(value, axis, pairs):
    return lax.ppermute(value, axis, pairs + [(j, i) for i, j in pairs])


def held_and_across(value, axis, size):
    held = value
    index = lax.axis_index(axis)
    step = 2
    while step < size:
        pairs = [(i, i + step) for i in range(step) if i + step < size]
        got = lax.ppermute(held, axis, pairs)
        held = jnp.where((index >= step) & (index < 2 * step), got, held)
        step *= 2
    return held, lax.ppermute(held, axis, [(i, i ^ 1) for i in range(size)])


def pick(parts, side, index):
    value = parts[-1][0]
    for array, _, *at in parts[:-1]:
        here = functools.reduce(jnp.logical_or, [index == position for position in at[side]])
        value = jnp.where(here, array, value)
    return value


def spread(value, index, size):
    held = value
    step = 2
    while step < size:
        pairs = [(i, i + step) for i in range(step) if i + step < size]
        got = lax.ppermute(held, "row", pairs)
        held = jnp.where((index >= step) & (index < 2 * step), got, held)
        step *= 2
    return held


def cross(value, size):
    return lax.ppermute(value, "row", [(i, i ^ 1) for i in range(size)])


def swap(value):
    return lax.ppermute(value, "depth", [(0, 1), (1, 0)])


def divisor(count, wanted):
    while count % wanted:
        wanted -= 1
    return wanted


def piece_sizes(count):
    if count == 12:
        return [1, 2, 3, 3, 3], [(0, 3), (3, 5)]
    return ([1, count - 1] if count > 1 else [1]), [(0, 2)]


def parts_of(own, swapped, offset, gone, back, turn):
    far = [((2,), (3,)), ((3,), (2,))]
    if turn:
        far.reverse()
    return [(own, 0, (0,), (1,)), (swapped, offset, (1,), (0,)), (gone, 0, *far[0]), (back, 0, *far[1])]


def plain_parts(arrays, size):
    even, odd = tuple(range(0, size, 2)), tuple(range(1, size, 2))
    return [(arrays[0], 0, even, odd), (arrays[1], 0, odd, even)]


def on_device(covariance):
    rows = lax.axis_size("row")
    cols = lax.axis_size("col")
    row, col, depth = (lax.axis_index(name) for name in ("row", "col", "depth"))
    place = jnp.stack([row, col, depth]).astype(jnp.int32)
    tile_rows, _, tile_cols, _, tile, _ = covariance.shape
    half = tile // 2
    zero = jnp.zeros((), jnp.int32)
    start = depth.astype(jnp.int32) * half

    def left(first, count):
        where = (zero + first, zero, zero, zero, start, zero)
        return lax.dynamic_slice(covariance, where, (count, 1, 1, 1, half, tile)).reshape(count, half, tile)

    def top(first, count):
        where = (zero, zero, zero + first, zero, start, zero)
        return lax.dynamic_slice(covariance, where, (1, 1, count, 1, half, tile)).reshape(count, half, tile)

    sizes, groups_at = piece_sizes(tile_rows)
    tall = cols == 4 and len(sizes) == 5
    mine = [left(sum(sizes[:i]), size) for i, size in enumerate(sizes)]
    turns = [i % 2 for i in range(len(sizes))]
    pairs = [(0, 1)], [(2, 3)]
    if tall:
        gone = [outward(mine[0], "col")]
        first_parts = parts_of(mine[0], exchange(mine[0], "col", pairs[0]), 0, gone[0], exchange(gone[0], "col", pairs[1]), 0)
        rest = left(1, tile_rows - 1)
    else:
        first_parts = plain_parts(held_and_across(mine[0], "col", cols), cols)

    top_parts = 3 if tile_cols % 3 == 0 else 1
    per_part = tile_cols // top_parts
    tops_held = [spread(top(0, per_part), row, rows)]
    pair = jnp.concatenate([pick(first_parts, side, col) for side in range(2)], 0)
    seed = spread(after(pair, tops_held[0]), row, rows)
    for part in range(1, top_parts):
        tops_held.append(spread(after(top(part * per_part, per_part), seed), row, rows))
    seed_across = cross(seed, rows)
    tops_across = [cross(after(tops_held[0], seed_across), rows)]
    seed_parts = [seed, seed_across, swap(seed), swap(seed_across)]
    if tall:
        gone.append(outward(after(mine[1], pair), "col", turns[1]))
        gone.append(outward(after(mine[2], seed), "col", turns[2]))
        seed_parts[3] = after(seed_parts[3], gone[1])
    matrix, inv = factor_start(place, seed_parts, half)
    stages = [matrix]
    for number, (begin, end) in enumerate(((half, tile), (tile, 2 * tile))):
        if tall:
            gone.append(outward(after(mine[3 + number], stages[number]), "col", turns[3 + number]))
            if number:
                matrix = after(matrix, gone[2])
        matrix, inv = factor_next(matrix, inv, begin, end, half)
        stages.append(matrix)
    for part in range(1, top_parts):
        tops_across.append(cross(after(tops_held[part], stages[part - 1]), rows))
    pieces = []
    for part in range(top_parts):
        waits = stages[min(part, 2)]
        pieces += [
            tops_held[part],
            tops_across[part],
            swap(after(tops_held[part], waits)),
            swap(after(tops_across[part], waits)),
        ]
    if tall:
        pieces[0] = after(pieces[0], gone[3])
    tops = columns(place, inv, pieces, top_parts, divisor(per_part, 2))

    groups = [(sizes[0], first_parts)]
    if tall:
        swapped = exchange(after(rest, stages[0]), "col", pairs[0])
        starts = (stages[0], stages[2], tops[1], gone[4])
        for number in range(1, len(sizes)):
            back = exchange(after(gone[number], starts[number - 1]), "col", pairs[1])
            offset = sum(sizes[1:number])
            own = after(mine[number], gone[4]) if number == 1 else mine[number]
            groups.append(
                (sizes[number], parts_of(own, swapped, offset, gone[number], back, turns[number]))
            )
    else:
        for number in range(1, len(sizes)):
            groups.append((sizes[number], plain_parts(held_and_across(mine[number], "col", cols), cols)))

    out = None
    group = divisor(tile_cols, 3)
    for begin, end in groups_at:
        first_tile = sum(sizes[:begin])
        out = update(place, inv, groups[begin:end], tops, covariance, out, first_tile, group)
    return out


def solution(mesh):
    in_specs = (P(None, "row", None, "col", None, None),)
    out_specs = P(None, "row", None, "col", "depth", None)
    return jax.shard_map(
        on_device, mesh=mesh, in_specs=in_specs, out_specs=out_specs, check_vma=False
    )
```

time: 724 us -> 167 us (0.23); the launches traced: 714 us -> 166 us
  waiting for transfers between devices: 429 us -> 12.1 us
  other arithmetic: 137 us -> 1.38 us
  starting transfers between devices: 0.13 us -> 72.5 us
  Pallas kernels: 0 us -> 70.1 us
  local copies, waits for them, and re-layouts: 72.6 us -> 9.9 us
  matrix products: 58.6 us -> 0 us
  between operations: 16.1 us -> 0.54 us
    psum x3 -> x0, waiting for transfers between devices: 414 us -> none  [spread(): return lax.psum(kept, axis)]
    another operation x17 -> x1, other arithmetic: 119 us -> 0.08 us  [on_device(): place = jnp.stack([row, col, depth]).astype(jnp.int32)]
    ppermute x0 -> x28, starting transfers between devices: none -> 72.5 us  [the longest x5 41 us: outward(): lax.ppermute(value, axis, [(0, 3), (1, 2)] if turn else [(0, 2), (1, 3)])]
    pallas_call x0 -> x6, Pallas kernels: none -> 70.1 us  [the longest x2 34.6 us: update(): pl.pallas_call(functools.partial(update_kernel, sources=len(cands), plan=...]
    dot_general x2 -> x0, matrix products: 50.2 us -> none  [the longest x1 34.6 us: on_device(): jnp.einsum('aik,bjk->abij', own_half, col_factor, precision=EXACT)]
    dynamic_slice x2 -> x0, local copies, waits for them, and re-layouts: 31.6 us -> none  [on_device(): lax.dynamic_slice_in_dim(local_tiles, depth_index * half_tile, half_tile, 2)]
    all_gather x1 -> x0, waiting for transfers between devices: 14.4 us -> none  [on_device(): lax.all_gather(partial_value[:, 0], 'depth', axis=1, tiled=True)]
    reshape x1 -> x5, local copies, waits for them, and re-layouts: 18.7 us -> 6.18 us  [the longest x4 4.68 us: left(): lax.dynamic_slice(covariance, where, (count, 1, 1, 1, half, tile))]
  transfers between devices with their start and end apart: 4 -> 28, of which waited for: 4 -> 6; matrix products, arithmetic and copies ran while one was open for 0% -> 4% of each run, Pallas kernels for 0% -> 32%
where the time goes in v1:
time: 167 us; the launch traced here: 166 us
  starting transfers between devices  72.5 us (43%)
  Pallas kernels  70.1 us (42%)
  waiting for transfers between devices  12.1 us (7%)
  local copies, waits for them, and re-layouts  9.9 us (6%)
    ppermute x5, starting transfers between devices, outward(): lax.ppermute(value, axis, [(0, 3), (1, 2)] if turn else [(0, 2), (1, 3)])  41 us
    pallas_call x2, Pallas kernels, update(): pl.pallas_call(functools.partial(update_kernel, sources=len(cands), plan=...  34.6 us
    pallas_call x2, Pallas kernels, factor_next(): pl.pallas_call(functools.partial(eliminate_kernel, start=start, stop=stop...  15.5 us
    pallas_call x1, Pallas kernels, columns(): pl.pallas_call(functools.partial(columns_kernel, parts=parts), out_shape=...  14 us
    ppermute x4, starting transfers between devices, spread(): got = lax.ppermute(held, 'row', pairs)  13.6 us
    ppermute x7, starting transfers between devices, exchange(): return lax.ppermute(value, axis, pairs + [(j, i) for i, j in pairs])  11.2 us
    ppermute x4, waiting for transfers between devices, spread(): got = lax.ppermute(held, 'row', pairs)  7.26 us
    pallas_call x1, Pallas kernels, factor_start(): pl.pallas_call(functools.partial(assemble_kernel, step=step), out_shape=[...  6.05 us
  transfers between devices with their start and end apart: 28, of which 6 were waited for; matrix products, arithmetic and copies ran while one was open for 4% of the time, Pallas kernels for 32%

profile of v1, /device:TPU:0, one launch (start us, length us, event | category | flops | bytes accessed | tf_op | source)
XLA Modules:
  0.0 166.5 jit_solution(10163605170775009903)
XLA Ops:
  0.0 0.9 dynamic-slice_bitcast_fusion.8.refs_0_
  0.9 5.9 %collective-permute-start = (f32[1,128,256]{2,1,0:T(8,128)S(1)}, f32[1,128,256]{2,1,0:T(8,128)S(1)}, u32[]{:S(2)}, u32[]{:S(2)}) collective-permute-start(f32[1,128,256]{2,1,0:T(8,128)S(1)} %dynamic-slice_bitcast_fusion.8.refs_0_), channel_id=1, source_target_pairs={{0,4},{2,6},{1,5},{3,7},{8,12},{10,14},{9,13},{11,15},{16,20},{18,... | collective-permute-start | bytes 393224 | tf_op jit(solution)/shard_map/ppermute | solution.py:328
  6.9 1.5 dynamic-slice_bitcast_fusion.1
  8.4 3.5 %collective-permute-start.3 = (f32[4,128,256]{2,1,0:T(8,128)S(1)}, f32[4,128,256]{2,1,0:T(8,128)S(1)}, u32[]{:S(2)}, u32[]{:S(2)}) collective-permute-start(f32[4,128,256]{2,1,0:T(8,128)S(1)} %get-tuple-element.76), channel_id=1, source_target_pairs={{0,16},{8,24},{1,17},{9,25},{2,18},{10,26},{3,19},{11,27},{4,20},{... | collective-permute-start | bytes 1572872 | tf_op jit(solution)/shard_map/ppermute | solution.py:360
  11.9 3.5 %collective-permute-start.1 = (f32[1,128,256]{2,1,0:T(8,128)S(1)}, f32[1,128,256]{2,1,0:T(8,128)S(1)}, u32[]{:S(2)}, u32[]{:S(2)}) collective-permute-start(f32[1,128,256]{2,1,0:T(8,128)S(1)} %dynamic-slice_bitcast_fusion.8.refs_0_), channel_id=1, source_target_pairs={{0,2},{2,0},{1,3},{3,1},{8,10},{10,8},{9,11},{11,9},{16,18},{18,16... | collective-permute-start | bytes 393224 | tf_op jit(solution)/shard_map/ppermute | solution.py:332
  15.4 0.7 collective-permute-start.2
  16.1 2.7 %collective-permute-done.1.refs_1_ = f32[1,128,256]{2,1,0:T(8,128)S(1)} collective-permute-done((f32[1,128,256]{2,1,0:T(8,128)S(1)}, f32[1,128,256]{2,1,0:T(8,128)S(1)}, u32[]{:S(2)}, u32[]{:S(2)}) %collective-permute-start.1) | collective-permute-done | bytes 131104 | tf_op jit(solution)/shard_map/ppermute | solution.py:332
  18.7 1.0 select_select_fusion.1
  19.8 2.9 %collective-permute-done.3 = f32[4,128,256]{2,1,0:T(8,128)S(1)} collective-permute-done((f32[4,128,256]{2,1,0:T(8,128)S(1)}, f32[4,128,256]{2,1,0:T(8,128)S(1)}, u32[]{:S(2)}, u32[]{:S(2)}) %collective-permute-start.3) | collective-permute-done | bytes 524320 | tf_op jit(solution)/shard_map/ppermute | solution.py:360
  22.8 4.4 %collective-permute-start.4 = (f32[2,128,256]{2,1,0:T(8,128)S(1)}, f32[2,128,256]{2,1,0:T(8,128)S(1)}, u32[]{:S(2)}, u32[]{:S(2)}) collective-permute-start(f32[2,128,256]{2,1,0:T(8,128)S(1)} %pad_maximum_fusion), channel_id=1, source_target_pairs={{0,16},{8,24},{1,17},{9,25},{2,18},{10,26},{3,19},{11,27},{4,20},{... | collective-permute-start | bytes 786440 | tf_op jit(solution)/shard_map/ppermute | solution.py:360
  27.2 4.3 %collective-permute-done.4 = f32[2,128,256]{2,1,0:T(8,128)S(1)} collective-permute-done((f32[2,128,256]{2,1,0:T(8,128)S(1)}, f32[2,128,256]{2,1,0:T(8,128)S(1)}, u32[]{:S(2)}, u32[]{:S(2)}) %collective-permute-start.4) | collective-permute-done | bytes 262176 | tf_op jit(solution)/shard_map/ppermute | solution.py:360
  31.6 1.6 collective-permute-start.5
  33.1 4.4 %collective-permute-start.15 = (f32[4,128,256]{2,1,0:T(8,128)S(1)}, f32[4,128,256]{2,1,0:T(8,128)S(1)}, u32[]{:S(2)}, u32[]{:S(2)}) collective-permute-start(f32[4,128,256]{2,1,0:T(8,128)S(1)} %get-tuple-element.54), channel_id=1, source_target_pairs={{0,16},{8,24},{1,17},{9,25},{2,18},{10,26},{3,19},{11,27},{4,20},{... | collective-permute-start | bytes 1572872 | tf_op jit(solution)/shard_map/ppermute | solution.py:360
  37.5 1.0 dynamic-slice_bitcast_fusion.7.refs_4_
  38.5 4.5 %collective-permute-start.8 = (f32[2,128,256]{2,1,0:T(8,128)S(1)}, f32[2,128,256]{2,1,0:T(8,128)}, u32[]{:S(2)}, u32[]{:S(2)}) collective-permute-start(f32[2,128,256]{2,1,0:T(8,128)S(1)} %dynamic-slice_bitcast_fusion.7.refs_4_), channel_id=1, source_target_pairs={{0,6},{2,4},{1,7},{3,5},{8,14},{10,12},{9,15},{11,13},{16,22},{18,... | collective-permute-start | bytes 786440 | tf_op jit(solution)/shard_map/ppermute | solution.py:328
  43.1 0.5 collective-permute-start.7
  43.6 1.3 dynamic-slice_bitcast_fusion.4
  44.9 2.0 %collective-permute-start.9 = (f32[3,128,256]{2,1,0:T(8,128)S(1)}, f32[3,128,256]{2,1,0:T(8,128)}, u32[]{:S(2)}, u32[]{:S(2)}) collective-permute-start(f32[3,128,256]{2,1,0:T(8,128)S(1)} %get-tuple-element.44.refs_8_), channel_id=1, source_target_pairs={{0,4},{2,6},{1,5},{3,7},{8,12},{10,14},{9,13},{11,15},{16,20},{18,... | collective-permute-start | bytes 1179656 | tf_op jit(solution)/shard_map/ppermute | solution.py:328
  47.0 1.3 collective-permute-start.19
  48.3 1.5 dynamic-slice_bitcast_fusion
  49.8 1.1 collective-permute-start.12
  51.0 6.0 %factor_start.1 = (f32[512,512]{1,0:T(8,128)S(1)}, f32[512,512]{1,0:T(8,128)S(1)}) custom-call(s32[3]{0:T(128)S(1)} %pad_add_fusion.place, f32[2,128,256]{2,1,0:T(8,128)S(1)} %broadcast_select_fusion.3.mine, f32[2,128,256]{2,1,0:T(8,128)S(1)} %collective-permute-done.5.across, f32[2,128,256]{2,1,0:T(8,128)S(1)} %collective-permute-done.6.mine_other, ...), custom_call_target="tpu_custom_call" | custom-call | flops 1 | bytes 1 | tf_op jit(solution)/shard_map/factor_start/pallas_call | solution.py:121
  57.1 5.1 %collective-permute-start.11 = (f32[3,128,256]{2,1,0:T(8,128)S(1)}, f32[3,128,256]{2,1,0:T(8,128)S(1)}, u32[]{:S(2)}, u32[]{:S(2)}) collective-permute-start(f32[3,128,256]{2,1,0:T(8,128)S(1)} %get-tuple-element.49.refs_0_), channel_id=1, source_target_pairs={{0,6},{2,4},{1,7},{3,5},{8,14},{10,12},{9,15},{11,13},{16,22},{18,... | collective-permute-start | bytes 1179656 | tf_op jit(solution)/shard_map/ppermute | solution.py:328
  62.2 1.6 collective-permute-start.16
  63.8 5.2 %factor_next.2 = (f32[512,512]{1,0:T(8,128)S(1)}, f32[512,512]{1,0:T(8,128)S(1)}) custom-call(f32[512,512]{1,0:T(8,128)S(1)} %get-tuple-element.41.matrix_in, f32[512,512]{1,0:T(8,128)S(1)} %get-tuple-element.42.inv_in), custom_call_target="tpu_custom_call" | custom-call | flops 1 | bytes 1 | tf_op jit(solution)/shard_map/factor_next/pallas_call | solution.py:136
  69.0 23.5 %collective-permute-start.24 = (f32[3,128,256]{2,1,0:T(8,128)S(1)}, f32[3,128,256]{2,1,0:T(8,128)}, u32[]{:S(2)}, u32[]{:S(2)}) collective-permute-start(f32[3,128,256]{2,1,0:T(8,128)S(1)} %get-tuple-element.65.refs_4_), channel_id=1, source_target_pairs={{0,4},{2,6},{1,5},{3,7},{8,12},{10,14},{9,13},{11,15},{16,20},{18,... | collective-permute-start | bytes 1179656 | tf_op jit(solution)/shard_map/ppermute | solution.py:328
  92.5 2.7 %collective-permute-start.10 = (f32[11,128,256]{2,1,0:T(8,128)S(1)}, f32[11,128,256]{2,1,0:T(8,128)S(1)}, u32[]{:S(2)}, u32[]{:S(2)}) collective-permute-start(f32[11,128,256]{2,1,0:T(8,128)S(1)} %dynamic-slice_bitcast_fusion), channel_id=1, source_target_pairs={{0,2},{2,0},{1,3},{3,1},{8,10},{10,8},{9,11},{11,9},{16,18},{18,16... | collective-permute-start | bytes 4325384 | tf_op jit(solution)/shard_map/ppermute | solution.py:332
  95.3 0.6 collective-permute-start.20
  95.9 10.2 %factor_next.3 = (f32[512,512]{1,0:T(8,128)}, f32[512,512]{1,0:T(8,128)S(1)}) custom-call(f32[512,512]{1,0:T(8,128)S(1)} %get-tuple-element.45.matrix_in, f32[512,512]{1,0:T(8,128)S(1)} %get-tuple-element.46.inv_in), custom_call_target="tpu_custom_call" | custom-call | flops 1 | bytes 1 | tf_op jit(solution)/shard_map/factor_next/pallas_call | solution.py:136
  106.1 1.0 copy-done
  107.1 0.5 collective-permute-start.21
  107.7 0.4 collective-permute-start.14
  108.1 0.9 collective-permute-done.13.refs_2_
  109.0 0.1 collective-permute-start.18
  109.1 0.6 collective-permute-done.21.refs_10_
  109.8 0.1 collective-permute-start.22
  109.9 0.6 collective-permute-done.17.refs_6_
  110.5 1.4 collective-permute-start.27
  111.9 0.7 collective-permute-start.26
  112.6 1.4 collective-permute-start.25
  114.1 0.8 copy-done.22
  115.0 14.0 %columns.1 = (bf16[1024,3072]{1,0:T(8,128)(2,1)}, f32[8,3072]{1,0:T(8,128)}) custom-call(s32[3]{0:T(128)} %copy-done.1, f32[512,512]{1,0:T(8,128)} %copy-done, f32[4,128,256]{2,1,0:T(8,128)} %copy-done.3, f32[4,128,256]{2,1,0:T(8,128)} %copy-done.14, f32[4,128,256]{2,1,0:T(8,128)} %copy-done.17, f32[4,128,256]{2,1,0:T(8,128)} %copy-done.20, ...), custom_call_target="tpu_custom_call" | custom-call | flops 1 | bytes 1 | tf_op jit(solution)/shard_map/columns/pallas_call | solution.py:188
  128.9 0.9 collective-permute-start.23
  130.0 0.6 copy-done.25
  130.6 0.5 copy-done.2
  131.1 17.3 %update.2.refs_10_ = f32[12,1,12,1,128,256]{5,4,3,2,1,0:T(8,128)} custom-call(s32[3]{0:T(128)} %copy-done.1, f32[512,512]{1,0:T(8,128)} %copy-done, f32[1,128,256]{2,1,0:T(8,128)} %copy-done.10, f32[1,128,256]{2,1,0:T(8,128)} %copy-done.12, f32[1,128,256]{2,1,0:T(8,128)} %copy-done.11, f32[1,128,256]{2,1,0:T(8,128)} %copy-done.13, f32[2,128,256]{2,1,0:T(8,128)} %copy-done.9, ...), custom_call_target="tpu_custom_call" | custom-call | flops 14495514624 | bytes 18874368 | tf_op jit(solution)/shard_map/update/pallas_call | solution.py:294
  148.4 0.7 copy-done.24
  149.2 17.3 %update.3 = f32[12,1,12,1,128,256]{5,4,3,2,1,0:T(8,128)} custom-call(s32[3]{0:T(128)} %copy-done.1, f32[512,512]{1,0:T(8,128)} %copy-done, f32[3,128,256]{2,1,0:T(8,128)} %copy-done.7, f32[11,128,256]{2,1,0:T(8,128)} %copy-done.2, f32[3,128,256]{2,1,0:T(8,128)} %copy-done.23, f32[3,128,256]{2,1,0:T(8,128)} %copy-done.24, ...), custom_call_target="tpu_custom_call", output_to_operand_aliasing={{}: (12, {})} | custom-call | flops 14495514624 | bytes 18874368 | tf_op jit(solution)/shard_map/update/pallas_call | solution.py:294
  (78 shorter events, 0.6 us)
Async XLA Ops:
  0.9 129.0 %copy-start.10 = (f32[1,128,256]{2,1,0:T(8,128)}, f32[1,128,256]{2,1,0:T(8,128)S(1)}, u32[]{:S(2)}) copy-start(f32[1,128,256]{2,1,0:T(8,128)S(1)} %dynamic-slice_bitcast_fusion.8.refs_0_) | copy-start | bytes 393220
  0.9 14.4 %collective-permute-start = (f32[1,128,256]{2,1,0:T(8,128)S(1)}, f32[1,128,256]{2,1,0:T(8,128)S(1)}, u32[]{:S(2)}, u32[]{:S(2)}) collective-permute-start(f32[1,128,256]{2,1,0:T(8,128)S(1)} %dynamic-slice_bitcast_fusion.8.refs_0_), channel_id=1, source_target_pairs={{0,4},{2,6},{1,5},{3,7},{8,12},{10,14},{9,13},{11,15},{16,20},{18,... | collective-permute-start | bytes 393224 | tf_op jit(solution)/shard_map/ppermute | solution.py:328
  8.4 14.3 %collective-permute-start.3 = (f32[4,128,256]{2,1,0:T(8,128)S(1)}, f32[4,128,256]{2,1,0:T(8,128)S(1)}, u32[]{:S(2)}, u32[]{:S(2)}) collective-permute-start(f32[4,128,256]{2,1,0:T(8,128)S(1)} %get-tuple-element.76), channel_id=1, source_target_pairs={{0,16},{8,24},{1,17},{9,25},{2,18},{10,26},{3,19},{11,27},{4,20},{... | collective-permute-start | bytes 1572872 | tf_op jit(solution)/shard_map/ppermute | solution.py:360
  11.9 6.9 %collective-permute-start.1 = (f32[1,128,256]{2,1,0:T(8,128)S(1)}, f32[1,128,256]{2,1,0:T(8,128)S(1)}, u32[]{:S(2)}, u32[]{:S(2)}) collective-permute-start(f32[1,128,256]{2,1,0:T(8,128)S(1)} %dynamic-slice_bitcast_fusion.8.refs_0_), channel_id=1, source_target_pairs={{0,2},{2,0},{1,3},{3,1},{8,10},{10,8},{9,11},{11,9},{16,18},{18,16... | collective-permute-start | bytes 393224 | tf_op jit(solution)/shard_map/ppermute | solution.py:332
  15.4 114.6 %copy-start.11 = (f32[1,128,256]{2,1,0:T(8,128)}, f32[1,128,256]{2,1,0:T(8,128)S(1)}, u32[]{:S(2)}) copy-start(f32[1,128,256]{2,1,0:T(8,128)S(1)} %collective-permute-done.refs_2_) | copy-start | bytes 393220
  15.4 3.4 %collective-permute-start.2 = (f32[1,128,256]{2,1,0:T(8,128)S(1)}, f32[1,128,256]{2,1,0:T(8,128)S(1)}, u32[]{:S(2)}, u32[]{:S(2)}) collective-permute-start(f32[1,128,256]{2,1,0:T(8,128)S(1)} %collective-permute-done.refs_2_), channel_id=1, source_target_pairs={{4,6},{6,4},{5,7},{7,5},{12,14},{14,12},{13,15},{15,13},{20,22},{2... | collective-permute-start | bytes 393224 | tf_op jit(solution)/shard_map/ppermute | solution.py:332
  18.7 111.2 %copy-start.12 = (f32[1,128,256]{2,1,0:T(8,128)}, f32[1,128,256]{2,1,0:T(8,128)S(1)}, u32[]{:S(2)}) copy-start(f32[1,128,256]{2,1,0:T(8,128)S(1)} %collective-permute-done.1.refs_1_) | copy-start | bytes 393220
  18.7 111.2 %copy-start.13 = (f32[1,128,256]{2,1,0:T(8,128)}, f32[1,128,256]{2,1,0:T(8,128)S(1)}, u32[]{:S(2)}) copy-start(f32[1,128,256]{2,1,0:T(8,128)S(1)} %collective-permute-done.2.refs_3_) | copy-start | bytes 393220
  22.8 92.1 %copy-start.3 = (f32[4,128,256]{2,1,0:T(8,128)}, f32[4,128,256]{2,1,0:T(8,128)S(1)}, u32[]{:S(2)}) copy-start(f32[4,128,256]{2,1,0:T(8,128)S(1)} %broadcast_select_fusion.2.refs_0_) | copy-start | bytes 1572868
  22.8 8.8 %collective-permute-start.4 = (f32[2,128,256]{2,1,0:T(8,128)S(1)}, f32[2,128,256]{2,1,0:T(8,128)S(1)}, u32[]{:S(2)}, u32[]{:S(2)}) collective-permute-start(f32[2,128,256]{2,1,0:T(8,128)S(1)} %pad_maximum_fusion), channel_id=1, source_target_pairs={{0,16},{8,24},{1,17},{9,25},{2,18},{10,26},{3,19},{11,27},{4,20},{... | collective-permute-start | bytes 786440 | tf_op jit(solution)/shard_map/ppermute | solution.py:360
  31.6 11.5 %collective-permute-start.5 = (f32[2,128,256]{2,1,0:T(8,128)S(1)}, f32[2,128,256]{2,1,0:T(8,128)S(1)}, u32[]{:S(2)}, u32[]{:S(2)}) collective-permute-start(f32[2,128,256]{2,1,0:T(8,128)S(1)} %broadcast_select_fusion.3.mine), channel_id=1, source_target_pairs={{0,8},{8,0},{16,24},{24,16},{1,9},{9,1},{17,25},{25,17},{2,10},{10... | collective-permute-start | bytes 786440 | tf_op jit(solution)/shard_map/ppermute | solution.py:367
  33.1 23.9 %collective-permute-start.15 = (f32[4,128,256]{2,1,0:T(8,128)S(1)}, f32[4,128,256]{2,1,0:T(8,128)S(1)}, u32[]{:S(2)}, u32[]{:S(2)}) collective-permute-start(f32[4,128,256]{2,1,0:T(8,128)S(1)} %get-tuple-element.54), channel_id=1, source_target_pairs={{0,16},{8,24},{1,17},{9,25},{2,18},{10,26},{3,19},{11,27},{4,20},{... | collective-permute-start | bytes 1572872 | tf_op jit(solution)/shard_map/ppermute | solution.py:360
  38.5 91.4 %copy-start.9 = (f32[2,128,256]{2,1,0:T(8,128)}, f32[2,128,256]{2,1,0:T(8,128)S(1)}, u32[]{:S(2)}) copy-start(f32[2,128,256]{2,1,0:T(8,128)S(1)} %dynamic-slice_bitcast_fusion.7.refs_4_) | copy-start | bytes 786436
  38.5 8.4 %collective-permute-start.8 = (f32[2,128,256]{2,1,0:T(8,128)S(1)}, f32[2,128,256]{2,1,0:T(8,128)}, u32[]{:S(2)}, u32[]{:S(2)}) collective-permute-start(f32[2,128,256]{2,1,0:T(8,128)S(1)} %dynamic-slice_bitcast_fusion.7.refs_4_), channel_id=1, source_target_pairs={{0,6},{2,4},{1,7},{3,5},{8,14},{10,12},{9,15},{11,13},{16,22},{18,... | collective-permute-start | bytes 786440 | tf_op jit(solution)/shard_map/ppermute | solution.py:328
  43.0 7.9 %collective-permute-start.6 = (f32[2,128,256]{2,1,0:T(8,128)S(1)}, f32[2,128,256]{2,1,0:T(8,128)S(1)}, u32[]{:S(2)}, u32[]{:S(2)}) collective-permute-start(f32[2,128,256]{2,1,0:T(8,128)S(1)} %broadcast_select_fusion.3.mine), channel_id=1, source_target_pairs={{0,1},{1,0},{2,3},{3,2},{4,5},{5,4},{6,7},{7,6},{8,9},{9,8},{10,11... | collective-permute-start | bytes 786440 | tf_op jit(solution)/shard_map/ppermute | solution.py:371
  43.1 6.8 %collective-permute-start.7 = (f32[2,128,256]{2,1,0:T(8,128)S(1)}, f32[2,128,256]{2,1,0:T(8,128)S(1)}, u32[]{:S(2)}, u32[]{:S(2)}) collective-permute-start(f32[2,128,256]{2,1,0:T(8,128)S(1)} %collective-permute-done.5.across), channel_id=1, source_target_pairs={{0,1},{1,0},{2,3},{3,2},{4,5},{5,4},{6,7},{7,6},{8,9},{9,8},{10,11... | collective-permute-start | bytes 786440 | tf_op jit(solution)/shard_map/ppermute | solution.py:371
  44.9 85.1 %copy-start.8 = (f32[3,128,256]{2,1,0:T(8,128)}, f32[3,128,256]{2,1,0:T(8,128)S(1)}, u32[]{:S(2)}) copy-start(f32[3,128,256]{2,1,0:T(8,128)S(1)} %get-tuple-element.44.refs_8_) | copy-start | bytes 1179652
  44.9 103.5 %copy-start.6 = (f32[3,128,256]{2,1,0:T(8,128)}, f32[3,128,256]{2,1,0:T(8,128)S(1)}, u32[]{:S(2)}) copy-start(f32[3,128,256]{2,1,0:T(8,128)S(1)} %get-tuple-element.65.refs_4_) | copy-start | bytes 1179652
  44.9 103.5 %copy-start.7 = (f32[3,128,256]{2,1,0:T(8,128)}, f32[3,128,256]{2,1,0:T(8,128)S(1)}, u32[]{:S(2)}) copy-start(f32[3,128,256]{2,1,0:T(8,128)S(1)} %get-tuple-element.49.refs_0_) | copy-start | bytes 1179652
  44.9 24.1 %collective-permute-start.9 = (f32[3,128,256]{2,1,0:T(8,128)S(1)}, f32[3,128,256]{2,1,0:T(8,128)}, u32[]{:S(2)}, u32[]{:S(2)}) collective-permute-start(f32[3,128,256]{2,1,0:T(8,128)S(1)} %get-tuple-element.44.refs_8_), channel_id=1, source_target_pairs={{0,4},{2,6},{1,5},{3,7},{8,12},{10,14},{9,13},{11,15},{16,20},{18,... | collective-permute-start | bytes 1179656 | tf_op jit(solution)/shard_map/ppermute | solution.py:328
  47.0 45.6 %collective-permute-start.19 = (f32[4,128,256]{2,1,0:T(8,128)S(1)}, f32[4,128,256]{2,1,0:T(8,128)S(1)}, u32[]{:S(2)}, u32[]{:S(2)}) collective-permute-start(f32[4,128,256]{2,1,0:T(8,128)S(1)} %get-tuple-element.58), channel_id=1, source_target_pairs={{0,16},{8,24},{1,17},{9,25},{2,18},{10,26},{3,19},{11,27},{4,20},{... | collective-permute-start | bytes 1572872 | tf_op jit(solution)/shard_map/ppermute | solution.py:360
  49.8 65.1 %copy-start.1 = (s32[3]{0:T(128)}, s32[3]{0:T(128)S(1)}, u32[]{:S(2)}) copy-start(s32[3]{0:T(128)S(1)} %pad_add_fusion.place) | copy-start | bytes 40
  49.8 45.4 %collective-permute-start.12 = (f32[4,128,256]{2,1,0:T(8,128)S(1)}, f32[4,128,256]{2,1,0:T(8,128)S(1)}, u32[]{:S(2)}, u32[]{:S(2)}) collective-permute-start(f32[4,128,256]{2,1,0:T(8,128)S(1)} %broadcast_select_fusion.2.refs_0_), channel_id=1, source_target_pairs={{0,8},{8,0},{16,24},{24,16},{1,9},{9,1},{17,25},{25,17},{2,10},{10... | collective-permute-start | bytes 1572872 | tf_op jit(solution)/shard_map/ppermute | solution.py:367
  57.1 57.8 %copy-start.4 = (f32[4,128,256]{2,1,0:T(8,128)}, f32[4,128,256]{2,1,0:T(8,128)S(1)}, u32[]{:S(2)}) copy-start(f32[4,128,256]{2,1,0:T(8,128)S(1)} %broadcast_select_fusion.1.refs_4_) | copy-start | bytes 1572868
  57.1 50.0 %collective-permute-start.11 = (f32[3,128,256]{2,1,0:T(8,128)S(1)}, f32[3,128,256]{2,1,0:T(8,128)S(1)}, u32[]{:S(2)}, u32[]{:S(2)}) collective-permute-start(f32[3,128,256]{2,1,0:T(8,128)S(1)} %get-tuple-element.49.refs_0_), channel_id=1, source_target_pairs={{0,6},{2,4},{1,7},{3,5},{8,14},{10,12},{9,15},{11,13},{16,22},{18,... | collective-permute-start | bytes 1179656 | tf_op jit(solution)/shard_map/ppermute | solution.py:328
  62.2 45.4 %collective-permute-start.16 = (f32[4,128,256]{2,1,0:T(8,128)S(1)}, f32[4,128,256]{2,1,0:T(8,128)S(1)}, u32[]{:S(2)}, u32[]{:S(2)}) collective-permute-start(f32[4,128,256]{2,1,0:T(8,128)S(1)} %broadcast_select_fusion.1.refs_4_), channel_id=1, source_target_pairs={{0,8},{8,0},{16,24},{24,16},{1,9},{9,1},{17,25},{25,17},{2,10},{10... | collective-permute-start | bytes 1572872 | tf_op jit(solution)/shard_map/ppermute | solution.py:367
  69.0 38.1 %collective-permute-start.24 = (f32[3,128,256]{2,1,0:T(8,128)S(1)}, f32[3,128,256]{2,1,0:T(8,128)}, u32[]{:S(2)}, u32[]{:S(2)}) collective-permute-start(f32[3,128,256]{2,1,0:T(8,128)S(1)} %get-tuple-element.65.refs_4_), channel_id=1, source_target_pairs={{0,4},{2,6},{1,5},{3,7},{8,12},{10,14},{9,13},{11,15},{16,20},{18,... | collective-permute-start | bytes 1179656 | tf_op jit(solution)/shard_map/ppermute | solution.py:328
  92.5 37.4 %collective-permute-start.10 = (f32[11,128,256]{2,1,0:T(8,128)S(1)}, f32[11,128,256]{2,1,0:T(8,128)S(1)}, u32[]{:S(2)}, u32[]{:S(2)}) collective-permute-start(f32[11,128,256]{2,1,0:T(8,128)S(1)} %dynamic-slice_bitcast_fusion), channel_id=1, source_target_pairs={{0,2},{2,0},{1,3},{3,1},{8,10},{10,8},{9,11},{11,9},{16,18},{18,16... | collective-permute-start | bytes 4325384 | tf_op jit(solution)/shard_map/ppermute | solution.py:332
  95.3 19.7 %copy-start.5 = (f32[4,128,256]{2,1,0:T(8,128)}, f32[4,128,256]{2,1,0:T(8,128)S(1)}, u32[]{:S(2)}) copy-start(f32[4,128,256]{2,1,0:T(8,128)S(1)} %broadcast_select_fusion.refs_8_) | copy-start | bytes 1572868
  95.3 19.6 %copy-start.14 = (f32[4,128,256]{2,1,0:T(8,128)}, f32[4,128,256]{2,1,0:T(8,128)S(1)}, u32[]{:S(2)}) copy-start(f32[4,128,256]{2,1,0:T(8,128)S(1)} %collective-permute-done.12.refs_1_) | copy-start | bytes 1572868
  95.3 12.4 %collective-permute-start.20 = (f32[4,128,256]{2,1,0:T(8,128)S(1)}, f32[4,128,256]{2,1,0:T(8,128)S(1)}, u32[]{:S(2)}, u32[]{:S(2)}) collective-permute-start(f32[4,128,256]{2,1,0:T(8,128)S(1)} %broadcast_select_fusion.refs_8_), channel_id=1, source_target_pairs={{0,8},{8,0},{16,24},{24,16},{1,9},{9,1},{17,25},{25,17},{2,10},{10... | collective-permute-start | bytes 1572872 | tf_op jit(solution)/shard_map/ppermute | solution.py:367
  107.1 7.0 %copy-start.23 = (f32[3,128,256]{2,1,0:T(8,128)}, f32[3,128,256]{2,1,0:T(8,128)S(1)}, u32[]{:S(2)}) copy-start(f32[3,128,256]{2,1,0:T(8,128)S(1)} %collective-permute-done.11.refs_2_) | copy-start | bytes 1179652
  107.1 1.9 %collective-permute-start.13 = (f32[4,128,256]{2,1,0:T(8,128)S(1)}, f32[4,128,256]{2,1,0:T(8,128)S(1)}, u32[]{:S(2)}, u32[]{:S(2)}) collective-permute-start(f32[4,128,256]{2,1,0:T(8,128)S(1)} %broadcast_select_fusion.2.refs_0_), channel_id=1, source_target_pairs={{0,1},{1,0},{2,3},{3,2},{4,5},{5,4},{6,7},{7,6},{8,9},{9,8},{10,11... | collective-permute-start | bytes 1572872 | tf_op jit(solution)/shard_map/ppermute | solution.py:371
  107.1 2.6 %collective-permute-start.21 = (f32[4,128,256]{2,1,0:T(8,128)S(1)}, f32[4,128,256]{2,1,0:T(8,128)S(1)}, u32[]{:S(2)}, u32[]{:S(2)}) collective-permute-start(f32[4,128,256]{2,1,0:T(8,128)S(1)} %broadcast_select_fusion.refs_8_), channel_id=1, source_target_pairs={{0,1},{1,0},{2,3},{3,2},{4,5},{5,4},{6,7},{7,6},{8,9},{9,8},{10,11... | collective-permute-start | bytes 1572872 | tf_op jit(solution)/shard_map/ppermute | solution.py:371
  107.6 7.3 %copy-start.15 = (f32[4,128,256]{2,1,0:T(8,128)}, f32[4,128,256]{2,1,0:T(8,128)S(1)}, u32[]{:S(2)}) copy-start(f32[4,128,256]{2,1,0:T(8,128)S(1)} %collective-permute-done.16.refs_5_) | copy-start | bytes 1572868
  107.6 2.9 %collective-permute-start.17 = (f32[4,128,256]{2,1,0:T(8,128)S(1)}, f32[4,128,256]{2,1,0:T(8,128)S(1)}, u32[]{:S(2)}, u32[]{:S(2)}) collective-permute-start(f32[4,128,256]{2,1,0:T(8,128)S(1)} %broadcast_select_fusion.1.refs_4_), channel_id=1, source_target_pairs={{0,1},{1,0},{2,3},{3,2},{4,5},{5,4},{6,7},{7,6},{8,9},{9,8},{10,11... | collective-permute-start | bytes 1572872 | tf_op jit(solution)/shard_map/ppermute | solution.py:371
  107.7 7.2 %copy-start.16 = (f32[4,128,256]{2,1,0:T(8,128)}, f32[4,128,256]{2,1,0:T(8,128)S(1)}, u32[]{:S(2)}) copy-start(f32[4,128,256]{2,1,0:T(8,128)S(1)} %collective-permute-done.20.refs_9_) | copy-start | bytes 1572868
  107.7 4.2 %collective-permute-start.14 = (f32[4,128,256]{2,1,0:T(8,128)S(1)}, f32[4,128,256]{2,1,0:T(8,128)S(1)}, u32[]{:S(2)}, u32[]{:S(2)}) collective-permute-start(f32[4,128,256]{2,1,0:T(8,128)S(1)} %collective-permute-done.12.refs_1_), channel_id=1, source_target_pairs={{0,1},{1,0},{2,3},{3,2},{4,5},{5,4},{6,7},{7,6},{8,9},{9,8},{10,11... | collective-permute-start | bytes 1572872 | tf_op jit(solution)/shard_map/ppermute | solution.py:371
  109.0 5.1 %copy-start.17 = (f32[4,128,256]{2,1,0:T(8,128)}, f32[4,128,256]{2,1,0:T(8,128)S(1)}, u32[]{:S(2)}) copy-start(f32[4,128,256]{2,1,0:T(8,128)S(1)} %collective-permute-done.13.refs_2_) | copy-start | bytes 1572868
  109.0 3.6 %collective-permute-start.18 = (f32[4,128,256]{2,1,0:T(8,128)S(1)}, f32[4,128,256]{2,1,0:T(8,128)S(1)}, u32[]{:S(2)}, u32[]{:S(2)}) collective-permute-start(f32[4,128,256]{2,1,0:T(8,128)S(1)} %collective-permute-done.16.refs_5_), channel_id=1, source_target_pairs={{0,1},{1,0},{2,3},{3,2},{4,5},{5,4},{6,7},{7,6},{8,9},{9,8},{10,11... | collective-permute-start | bytes 1572872 | tf_op jit(solution)/shard_map/ppermute | solution.py:371
  109.8 4.3 %copy-start.18 = (f32[4,128,256]{2,1,0:T(8,128)}, f32[4,128,256]{2,1,0:T(8,128)S(1)}, u32[]{:S(2)}) copy-start(f32[4,128,256]{2,1,0:T(8,128)S(1)} %collective-permute-done.21.refs_10_) | copy-start | bytes 1572868
  109.8 4.3 %collective-permute-start.22 = (f32[4,128,256]{2,1,0:T(8,128)S(1)}, f32[4,128,256]{2,1,0:T(8,128)S(1)}, u32[]{:S(2)}, u32[]{:S(2)}) collective-permute-start(f32[4,128,256]{2,1,0:T(8,128)S(1)} %collective-permute-done.20.refs_9_), channel_id=1, source_target_pairs={{0,1},{1,0},{2,3},{3,2},{4,5},{5,4},{6,7},{7,6},{8,9},{9,8},{10,11... | collective-permute-start | bytes 1572872 | tf_op jit(solution)/shard_map/ppermute | solution.py:371
  110.5 3.6 %copy-start.19 = (f32[4,128,256]{2,1,0:T(8,128)}, f32[4,128,256]{2,1,0:T(8,128)S(1)}, u32[]{:S(2)}) copy-start(f32[4,128,256]{2,1,0:T(8,128)S(1)} %collective-permute-done.17.refs_6_) | copy-start | bytes 1572868
  110.5 19.4 %collective-permute-start.27 = (f32[3,128,256]{2,1,0:T(8,128)}, f32[3,128,256]{2,1,0:T(8,128)}, u32[]{:S(2)}, u32[]{:S(2)}) collective-permute-start(f32[3,128,256]{2,1,0:T(8,128)} %collective-permute-done.9.refs_9_), channel_id=1, source_target_pairs={{4,6},{6,4},{5,7},{7,5},{12,14},{14,12},{13,15},{15,13},{20,22},{2... | collective-permute-start | bytes 1179656 | tf_op jit(solution)/shard_map/ppermute | solution.py:332
  111.9 2.2 %copy-start.20 = (f32[4,128,256]{2,1,0:T(8,128)}, f32[4,128,256]{2,1,0:T(8,128)S(1)}, u32[]{:S(2)}) copy-start(f32[4,128,256]{2,1,0:T(8,128)S(1)} %collective-permute-done.14.refs_3_) | copy-start | bytes 1572868
  111.9 17.9 %collective-permute-start.26 = (f32[2,128,256]{2,1,0:T(8,128)}, f32[2,128,256]{2,1,0:T(8,128)S(1)}, u32[]{:S(2)}, u32[]{:S(2)}) collective-permute-start(f32[2,128,256]{2,1,0:T(8,128)} %collective-permute-done.8.refs_6_), channel_id=1, source_target_pairs={{4,6},{6,4},{5,7},{7,5},{12,14},{14,12},{13,15},{15,13},{20,22},{2... | collective-permute-start | bytes 786440 | tf_op jit(solution)/shard_map/ppermute | solution.py:332
  112.6 35.8 %collective-permute-start.25 = (f32[3,128,256]{2,1,0:T(8,128)}, f32[3,128,256]{2,1,0:T(8,128)}, u32[]{:S(2)}, u32[]{:S(2)}) collective-permute-start(f32[3,128,256]{2,1,0:T(8,128)} %collective-permute-done.24.refs_5_), channel_id=1, source_target_pairs={{4,6},{6,4},{5,7},{7,5},{12,14},{14,12},{13,15},{15,13},{20,22},{2... | collective-permute-start | bytes 1179656 | tf_op jit(solution)/shard_map/ppermute | solution.py:332
  128.9 19.5 %collective-permute-start.23 = (f32[3,128,256]{2,1,0:T(8,128)}, f32[3,128,256]{2,1,0:T(8,128)S(1)}, u32[]{:S(2)}, u32[]{:S(2)}) collective-permute-start(f32[3,128,256]{2,1,0:T(8,128)} %copy-done.23), channel_id=1, source_target_pairs={{4,6},{6,4},{5,7},{7,5},{12,14},{14,12},{13,15},{15,13},{20,22},{2... | collective-permute-start | bytes 1179656 | tf_op jit(solution)/shard_map/ppermute | solution.py:332
  (6 other events, 5.9 us)

commit v2 on v1

--- a/solution.py
+++ b/solution.py
@@ -13,6 +13,7 @@
 LIMIT = 56 << 20
 ANY = pl.BlockSpec(memory_space=pl.ANY)
 LIGHT = pl.CostEstimate(flops=1, bytes_accessed=1, transcendentals=0)
+HEAVY = pl.CostEstimate(flops=10**10, bytes_accessed=1, transcendentals=0)
 
 
 def dot(a, b, ca=1, cb=0, precision=None):
@@ -139,7 +140,7 @@
         in_specs=[whole] * 2,
         out_specs=[whole] * 2,
         compiler_params=pltpu.CompilerParams(vmem_limit_bytes=16 << 20),
-        cost_estimate=LIGHT,
+        cost_estimate=HEAVY if stop == n else LIGHT,
         name="factor_next",
     )(matrix, inv)
 
@@ -203,7 +204,7 @@
             scratch_shapes=[pltpu.VMEM((n, width), F32)],
         ),
         compiler_params=pltpu.CompilerParams(vmem_limit_bytes=LIMIT),
-        cost_estimate=LIGHT,
+        cost_estimate=HEAVY,
         name="columns",
     )(place, inv, *pieces)
 
@@ -379,7 +380,7 @@
 
 def piece_sizes(count):
     if count == 12:
-        return [1, 2, 3, 3, 3], [(0, 3), (3, 5)]
+        return [1, 7, 4], [(0, 2), (2, 3)]
     return ([1, count - 1] if count > 1 else [1]), [(0, 2)]
 
 
@@ -414,18 +415,17 @@
         return lax.dynamic_slice(covariance, where, (1, 1, count, 1, half, tile)).reshape(count, half, tile)
 
     sizes, groups_at = piece_sizes(tile_rows)
-    tall = cols == 4 and len(sizes) == 5
+    tall = cols == 4 and len(sizes) == 3
     mine = [left(sum(sizes[:i]), size) for i, size in enumerate(sizes)]
     turns = [i % 2 for i in range(len(sizes))]
     pairs = [(0, 1)], [(2, 3)]
     if tall:
         gone = [outward(mine[0], "col")]
         first_parts = parts_of(mine[0], exchange(mine[0], "col", pairs[0]), 0, gone[0], exchange(gone[0], "col", pairs[1]), 0)
-        rest = left(1, tile_rows - 1)
     else:
         first_parts = plain_parts(held_and_across(mine[0], "col", cols), cols)
 
-    top_parts = 3 if tile_cols % 3 == 0 else 1
+    top_parts = 2 if tile_cols % 2 == 0 else 1
     per_part = tile_cols // top_parts
     tops_held = [spread(top(0, per_part), row, rows)]
     pair = jnp.concatenate([pick(first_parts, side, col) for side in range(2)], 0)
@@ -437,49 +437,44 @@
     seed_parts = [seed, seed_across, swap(seed), swap(seed_across)]
     if tall:
         gone.append(outward(after(mine[1], pair), "col", turns[1]))
-        gone.append(outward(after(mine[2], seed), "col", turns[2]))
-        seed_parts[3] = after(seed_parts[3], gone[1])
     matrix, inv = factor_start(place, seed_parts, half)
     stages = [matrix]
-    for number, (begin, end) in enumerate(((half, tile), (tile, 2 * tile))):
-        if tall:
-            gone.append(outward(after(mine[3 + number], stages[number]), "col", turns[3 + number]))
-            if number:
-                matrix = after(matrix, gone[2])
+    for begin, end in ((half, tile), (tile, 2 * tile)):
         matrix, inv = factor_next(matrix, inv, begin, end, half)
         stages.append(matrix)
     for part in range(1, top_parts):
         tops_across.append(cross(after(tops_held[part], stages[part - 1]), rows))
     pieces = []
     for part in range(top_parts):
-        waits = stages[min(part, 2)]
+        waits = stages[2 * min(part, 1)]
         pieces += [
             tops_held[part],
             tops_across[part],
             swap(after(tops_held[part], waits)),
             swap(after(tops_across[part], waits)),
         ]
-    if tall:
-        pieces[0] = after(pieces[0], gone[3])
-    tops = columns(place, inv, pieces, top_parts, divisor(per_part, 2))
-
     groups = [(sizes[0], first_parts)]
     if tall:
-        swapped = exchange(after(rest, stages[0]), "col", pairs[0])
-        starts = (stages[0], stages[2], tops[1], gone[4])
-        for number in range(1, len(sizes)):
-            back = exchange(after(gone[number], starts[number - 1]), "col", pairs[1])
-            offset = sum(sizes[1:number])
-            own = after(mine[number], gone[4]) if number == 1 else mine[number]
-            groups.append(
-                (sizes[number], parts_of(own, swapped, offset, gone[number], back, turns[number]))
-            )
+        arrived = after(gone[1], stages[2])
+        gone.append(outward(after(mine[2], arrived), "col", turns[2]))
+        first, second = (0, 3), (1, 2)
+        held = jnp.where(col < 2, mine[1], arrived)
+        across = exchange(held, "col", pairs[0] + pairs[1])
+        groups.append((sizes[1], [(held, 0, first, second), (across, 0, second, first)]))
+        pieces[0] = after(pieces[0], held)
     else:
         for number in range(1, len(sizes)):
             groups.append((sizes[number], plain_parts(held_and_across(mine[number], "col", cols), cols)))
-
+    tops = columns(place, inv, pieces, top_parts, divisor(per_part, 2))
+    if tall:
+        arrived = after(gone[2], tops[1], across)
+        first, second = (0, 2), (1, 3)
+        held = jnp.where(col < 2, mine[2], arrived)
+        across = exchange(held, "col", pairs[0] + pairs[1])
+        groups.append((sizes[2], [(held, 0, first, second), (across, 0, second, first)]))
+        groups[0] = (sizes[0], [(after(first_parts[0][0], held), *first_parts[0][1:]), *first_parts[1:]])
     out = None
-    group = divisor(tile_cols, 3)
+    group = divisor(tile_cols, 2)
     for begin, end in groups_at:
         first_tile = sum(sizes[:begin])
         out = update(place, inv, groups[begin:end], tops, covariance, out, first_tile, group)

time: 167 us -> 160 us (0.958)
  starting transfers between devices: 72.5 us -> 38.6 us
  waiting for transfers between devices: 12.1 us -> 39.3 us
  other arithmetic: 1.38 us -> 5.01 us
  local copies, waits for them, and re-layouts: 9.9 us -> 6.54 us
    ppermute x5 -> x3, starting transfers between devices: 41 us -> 14.3 us  [outward(): lax.ppermute(value, axis, [(0, 3), (1, 2)] if turn else [(0, 2), (1, 3)])]
    ppermute x4 -> x3, waiting for transfers between devices: 0.01 us -> 15.2 us  [cross(): return lax.ppermute(value, 'row', [(i, i ^ 1) for i in range(size)])]
    ppermute x5 -> x3, waiting for transfers between devices: 0.01 us -> 13.4 us  [outward(): lax.ppermute(value, axis, [(0, 3), (1, 2)] if turn else [(0, 2), (1, 3)])]
    ppermute x7 -> x4, starting transfers between devices: 11.2 us -> 6.22 us  [exchange(): return lax.ppermute(value, axis, pairs + [(j, i) for i, j in pairs])]
    select_n x0 -> x2, other arithmetic: none -> 2.76 us  [the longest x1 1.44 us: on_device(): held = jnp.where(col < 2, mine[2], arrived)]
    ppermute x8 -> x6, waiting for transfers between devices: 2.11 us -> 0.02 us  [swap(): return lax.ppermute(value, 'depth', [(0, 1), (1, 0)])]
    unnamed x52 -> x22, local copies, waits for them, and re-layouts: 3.73 us -> 1.82 us
    reshape x4 -> x3, local copies, waits for them, and re-layouts: 4.68 us -> 3.24 us  [left(): lax.dynamic_slice(covariance, where, (count, 1, 1, 1, half, tile))]
  transfers between devices with their start and end apart: 28 -> 19, of which waited for: 6 -> 6; matrix products, arithmetic and copies ran while one was open for 4% -> 4% of each run, Pallas kernels for 32% -> 35%
where the time goes in v2:
time: 160 us; the launch traced here: 159 us
  Pallas kernels  69.6 us (43%)
  waiting for transfers between devices  39.3 us (25%)
  starting transfers between devices  38.6 us (24%)
  local copies, waits for them, and re-layouts  6.54 us (4%)
  other arithmetic  5.01 us (3%)
    pallas_call x2, Pallas kernels, update(): pl.pallas_call(functools.partial(update_kernel, sources=len(cands), plan=...  34.5 us
    pallas_call x2, Pallas kernels, factor_next(): pl.pallas_call(functools.partial(eliminate_kernel, start=start, stop=stop...  15.7 us
    ppermute x3, waiting for transfers between devices, cross(): return lax.ppermute(value, 'row', [(i, i ^ 1) for i in range(size)])  15.2 us
    ppermute x3, starting transfers between devices, outward(): lax.ppermute(value, axis, [(0, 3), (1, 2)] if turn else [(0, 2), (1, 3)])  14.3 us
    ppermute x3, starting transfers between devices, spread(): got = lax.ppermute(held, 'row', pairs)  13.8 us
    ppermute x3, waiting for transfers between devices, outward(): lax.ppermute(value, axis, [(0, 3), (1, 2)] if turn else [(0, 2), (1, 3)])  13.4 us
    pallas_call x1, Pallas kernels, columns(): pl.pallas_call(functools.partial(columns_kernel, parts=parts), out_shape=...  13.4 us
    ppermute x3, waiting for transfers between devices, spread(): got = lax.ppermute(held, 'row', pairs)  8.01 us
  transfers between devices with their start and end apart: 19, of which 6 were waited for; matrix products, arithmetic and copies ran while one was open for 4% of the time, Pallas kernels for 35%

profile of v2, /device:TPU:0, one launch (start us, length us, event | category | flops | bytes accessed | tf_op | source)
XLA Modules:
  0.0 159.3 jit_solution(7879776553556910267)
XLA Ops:
  0.0 1.5 dynamic-slice_bitcast_fusion.1
  1.5 4.9 %collective-permute-start.3 = (f32[6,128,256]{2,1,0:T(8,128)S(1)}, f32[6,128,256]{2,1,0:T(8,128)S(1)}, u32[]{:S(2)}, u32[]{:S(2)}) collective-permute-start(f32[6,128,256]{2,1,0:T(8,128)S(1)} %get-tuple-element.50), channel_id=1, source_target_pairs={{0,16},{8,24},{1,17},{9,25},{2,18},{10,26},{3,19},{11,27},{4,20},{... | collective-permute-start | bytes 2359304 | tf_op jit(solution)/shard_map/ppermute | solution.py:361
  6.4 0.9 dynamic-slice_bitcast_fusion.4.refs_0_
  7.3 4.5 %collective-permute-start = (f32[1,128,256]{2,1,0:T(8,128)S(1)}, f32[1,128,256]{2,1,0:T(8,128)S(1)}, u32[]{:S(2)}, u32[]{:S(2)}) collective-permute-start(f32[1,128,256]{2,1,0:T(8,128)S(1)} %dynamic-slice_bitcast_fusion.4.refs_0_), channel_id=1, source_target_pairs={{0,4},{2,6},{1,5},{3,7},{8,12},{10,14},{9,13},{11,15},{16,20},{18,... | collective-permute-start | bytes 393224 | tf_op jit(solution)/shard_map/ppermute | solution.py:329
  11.8 3.5 %collective-permute-start.1 = (f32[1,128,256]{2,1,0:T(8,128)S(1)}, f32[1,128,256]{2,1,0:T(8,128)S(1)}, u32[]{:S(2)}, u32[]{:S(2)}) collective-permute-start(f32[1,128,256]{2,1,0:T(8,128)S(1)} %dynamic-slice_bitcast_fusion.4.refs_0_), channel_id=1, source_target_pairs={{0,2},{2,0},{1,3},{3,1},{8,10},{10,8},{9,11},{11,9},{16,18},{18,16... | collective-permute-start | bytes 393224 | tf_op jit(solution)/shard_map/ppermute | solution.py:333
  15.3 0.0 collective-permute-done.refs_2_
  15.4 0.7 collective-permute-start.2
  16.1 2.7 %collective-permute-done.1.refs_1_ = f32[1,128,256]{2,1,0:T(8,128)S(1)} collective-permute-done((f32[1,128,256]{2,1,0:T(8,128)S(1)}, f32[1,128,256]{2,1,0:T(8,128)S(1)}, u32[]{:S(2)}, u32[]{:S(2)}) %collective-permute-start.1) | collective-permute-done | bytes 131104 | tf_op jit(solution)/shard_map/ppermute | solution.py:333
  18.7 0.0 collective-permute-done.2.refs_3_
  18.7 1.0 select_select_fusion.1
  19.8 3.3 %collective-permute-done.3 = f32[6,128,256]{2,1,0:T(8,128)S(1)} collective-permute-done((f32[6,128,256]{2,1,0:T(8,128)S(1)}, f32[6,128,256]{2,1,0:T(8,128)S(1)}, u32[]{:S(2)}, u32[]{:S(2)}) %collective-permute-start.3) | collective-permute-done | bytes 786464 | tf_op jit(solution)/shard_map/ppermute | solution.py:361
  23.1 0.1 broadcast_select_fusion.2.refs_0_
  23.3 4.4 %collective-permute-start.4 = (f32[2,128,256]{2,1,0:T(8,128)S(1)}, f32[2,128,256]{2,1,0:T(8,128)S(1)}, u32[]{:S(2)}, u32[]{:S(2)}) collective-permute-start(f32[2,128,256]{2,1,0:T(8,128)S(1)} %pad_maximum_fusion), channel_id=1, source_target_pairs={{0,16},{8,24},{1,17},{9,25},{2,18},{10,26},{3,19},{11,27},{4,20},{... | collective-permute-start | bytes 786440 | tf_op jit(solution)/shard_map/ppermute | solution.py:361
  27.7 4.7 %collective-permute-done.4 = f32[2,128,256]{2,1,0:T(8,128)S(1)} collective-permute-done((f32[2,128,256]{2,1,0:T(8,128)S(1)}, f32[2,128,256]{2,1,0:T(8,128)S(1)}, u32[]{:S(2)}, u32[]{:S(2)}) %collective-permute-start.4) | collective-permute-done | bytes 262176 | tf_op jit(solution)/shard_map/ppermute | solution.py:361
  32.4 4.4 %collective-permute-start.13 = (f32[6,128,256]{2,1,0:T(8,128)S(1)}, f32[6,128,256]{2,1,0:T(8,128)S(1)}, u32[]{:S(2)}, u32[]{:S(2)}) collective-permute-start(f32[6,128,256]{2,1,0:T(8,128)S(1)} %get-tuple-element.41), channel_id=1, source_target_pairs={{0,16},{8,24},{1,17},{9,25},{2,18},{10,26},{3,19},{11,27},{4,20},{... | collective-permute-start | bytes 2359304 | tf_op jit(solution)/shard_map/ppermute | solution.py:361
  36.8 1.6 collective-permute-start.5
  38.4 4.9 %collective-permute-done.5.across = f32[2,128,256]{2,1,0:T(8,128)S(1)} collective-permute-done((f32[2,128,256]{2,1,0:T(8,128)S(1)}, f32[2,128,256]{2,1,0:T(8,128)S(1)}, u32[]{:S(2)}, u32[]{:S(2)}) %collective-permute-start.5) | collective-permute-done | bytes 262176 | tf_op jit(solution)/shard_map/ppermute | solution.py:368
  43.2 0.0 collective-permute-start.7
  43.3 0.1 pad_add_fusion.place
  43.3 1.2 dynamic-slice_bitcast_fusion
  44.6 6.0 %collective-permute-start.8 = (f32[7,128,256]{2,1,0:T(8,128)S(1)}, f32[7,128,256]{2,1,0:T(8,128)S(1)}, u32[]{:S(2)}, u32[]{:S(2)}) collective-permute-start(f32[7,128,256]{2,1,0:T(8,128)S(1)} %dynamic-slice_bitcast_fusion), channel_id=1, source_target_pairs={{0,6},{2,4},{1,7},{3,5},{8,14},{10,12},{9,15},{11,13},{16,22},{18,... | collective-permute-start | bytes 2752520 | tf_op jit(solution)/shard_map/ppermute | solution.py:329
  50.5 1.6 collective-permute-start.10
  52.1 0.0 collective-permute-done.6.mine_other
  52.1 0.0 collective-permute-done.7.across_other
  52.1 6.0 %factor_start.1 = (f32[512,512]{1,0:T(8,128)S(1)}, f32[512,512]{1,0:T(8,128)S(1)}) custom-call(s32[3]{0:T(128)S(1)} %pad_add_fusion.place, f32[2,128,256]{2,1,0:T(8,128)S(1)} %broadcast_select_fusion.4.mine, f32[2,128,256]{2,1,0:T(8,128)S(1)} %collective-permute-done.5.across, f32[2,128,256]{2,1,0:T(8,128)S(1)} %collective-permute-done.6.mine_other, ...), custom_call_target="tpu_custom_call" | custom-call | flops 1 | bytes 1 | tf_op jit(solution)/shard_map/factor_start/pallas_call | solution.py:122
  58.1 0.1 collective-permute-start.11
  58.2 5.2 %factor_next.2 = (f32[512,512]{1,0:T(8,128)S(1)}, f32[512,512]{1,0:T(8,128)S(1)}) custom-call(f32[512,512]{1,0:T(8,128)S(1)} %get-tuple-element.28.matrix_in, f32[512,512]{1,0:T(8,128)S(1)} %get-tuple-element.29.inv_in), custom_call_target="tpu_custom_call" | custom-call | flops 1 | bytes 1 | tf_op jit(solution)/shard_map/factor_next/pallas_call | solution.py:137
  63.5 1.0 broadcast_select_fusion.1.refs_4_
  64.5 0.5 collective-permute-start.14
  65.0 10.4 %factor_next.3 = (f32[512,512]{1,0:T(8,128)}, f32[512,512]{1,0:T(8,128)S(1)}) custom-call(f32[512,512]{1,0:T(8,128)S(1)} %get-tuple-element.30.matrix_in, f32[512,512]{1,0:T(8,128)S(1)} %get-tuple-element.31.inv_in), custom_call_target="tpu_custom_call" | custom-call | flops 10000000000 | bytes 1 | tf_op jit(solution)/shard_map/factor_next/pallas_call | solution.py:137
  75.4 1.0 copy-done
  76.4 0.2 collective-permute-start.15
  76.6 0.3 collective-permute-start.12
  76.9 10.3 %collective-permute-done.14.refs_5_ = f32[6,128,256]{2,1,0:T(8,128)} collective-permute-done((f32[6,128,256]{2,1,0:T(8,128)}, f32[6,128,256]{2,1,0:T(8,128)}, u32[]{:S(2)}, u32[]{:S(2)}) %collective-permute-start.14) | collective-permute-done | bytes 786464 | tf_op jit(solution)/shard_map/ppermute | solution.py:368
  87.2 0.0 collective-permute-start.16
  87.2 1.1 dynamic-slice_bitcast_fusion.3
  88.3 0.0 collective-permute-done.8
  88.3 1.3 broadcast_select_fusion.refs_4_
  89.7 2.0 %collective-permute-start.17 = (f32[7,128,256]{2,1,0:T(8,128)S(1)}, f32[7,128,256]{2,1,0:T(8,128)S(1)}, u32[]{:S(2)}, u32[]{:S(2)}) collective-permute-start(f32[7,128,256]{2,1,0:T(8,128)S(1)} %broadcast_select_fusion.refs_4_), channel_id=1, source_target_pairs={{0,2},{4,6},{2,0},{6,4},{1,3},{5,7},{3,1},{7,5},{8,10},{12,14},{10... | collective-permute-start | bytes 2752520 | tf_op jit(solution)/shard_map/ppermute | solution.py:333
  91.7 0.0 collective-permute-done.11.refs_2_
  91.7 3.9 %collective-permute-start.9 = (f32[4,128,256]{2,1,0:T(8,128)S(1)}, f32[4,128,256]{2,1,0:T(8,128)S(1)}, u32[]{:S(2)}, u32[]{:S(2)}) collective-permute-start(f32[4,128,256]{2,1,0:T(8,128)S(1)} %dynamic-slice_bitcast_fusion.3), channel_id=1, source_target_pairs={{0,4},{2,6},{1,5},{3,7},{8,12},{10,14},{9,13},{11,15},{16,20},{18,... | collective-permute-start | bytes 1572872 | tf_op jit(solution)/shard_map/ppermute | solution.py:329
  95.6 13.4 %columns.1 = (bf16[1024,3072]{1,0:T(8,128)(2,1)}, f32[8,3072]{1,0:T(8,128)}) custom-call(s32[3]{0:T(128)} %copy-done.1, f32[512,512]{1,0:T(8,128)} %copy-done, f32[6,128,256]{2,1,0:T(8,128)} %copy-done.4, f32[6,128,256]{2,1,0:T(8,128)} %collective-permute-done.10.refs_1_, f32[6,128,256]{2,1,0:T(8,128)} %collective-permute-done.11.refs_2_, ...), custom_call_target="tpu_custom_call" | custom-call | flops 10000000000 | bytes 1 | tf_op jit(solution)/shard_map/columns/pallas_call | solution.py:189
  109.0 13.4 %collective-permute-done.9 = f32[4,128,256]{2,1,0:T(8,128)S(1)} collective-permute-done((f32[4,128,256]{2,1,0:T(8,128)S(1)}, f32[4,128,256]{2,1,0:T(8,128)S(1)}, u32[]{:S(2)}, u32[]{:S(2)}) %collective-permute-start.9) | collective-permute-done | bytes 524320 | tf_op jit(solution)/shard_map/ppermute | solution.py:329
  122.4 1.4 broadcast_select_fusion.3.refs_0_
  123.8 0.1 collective-permute-start.18
  123.9 20.8 %update.2.refs_5_ = f32[12,1,12,1,128,256]{5,4,3,2,1,0:T(8,128)} custom-call(s32[3]{0:T(128)} %copy-done.1, f32[512,512]{1,0:T(8,128)} %copy-done, f32[1,128,256]{2,1,0:T(8,128)} %copy-done.6, f32[1,128,256]{2,1,0:T(8,128)} %copy-done.8, f32[1,128,256]{2,1,0:T(8,128)} %copy-done.7, f32[1,128,256]{2,1,0:T(8,128)} %copy-done.9, f32[7,128,256]{2,1,0:T(8,128)} %copy-done.3, ...), custom_call_target="tpu_custom_call" | custom-call | flops 19327352832 | bytes 25165824 | tf_op jit(solution)/shard_map/update/pallas_call | solution.py:295
  144.8 0.8 copy-done.5
  145.6 13.6 %update.3 = f32[12,1,12,1,128,256]{5,4,3,2,1,0:T(8,128)} custom-call(s32[3]{0:T(128)} %copy-done.1, f32[512,512]{1,0:T(8,128)} %copy-done, f32[4,128,256]{2,1,0:T(8,128)} %copy-done.2, f32[4,128,256]{2,1,0:T(8,128)} %copy-done.5, bf16[1024,3072]{1,0:T(8,128)(2,1)} %get-tuple-element.47.refs_6_.refs_2_, ...), custom_call_target="tpu_custom_call", output_to_operand_aliasing={{}: (7, {})} | custom-call | flops 9663676416 | bytes 12582912 | tf_op jit(solution)/shard_map/update/pallas_call | solution.py:295
  (30 shorter events, 0.1 us)
Async XLA Ops:
  1.5 21.7 %collective-permute-start.3 = (f32[6,128,256]{2,1,0:T(8,128)S(1)}, f32[6,128,256]{2,1,0:T(8,128)S(1)}, u32[]{:S(2)}, u32[]{:S(2)}) collective-permute-start(f32[6,128,256]{2,1,0:T(8,128)S(1)} %get-tuple-element.50), channel_id=1, source_target_pairs={{0,16},{8,24},{1,17},{9,25},{2,18},{10,26},{3,19},{11,27},{4,20},{... | collective-permute-start | bytes 2359304 | tf_op jit(solution)/shard_map/ppermute | solution.py:361
  7.3 101.7 %copy-start.6 = (f32[1,128,256]{2,1,0:T(8,128)}, f32[1,128,256]{2,1,0:T(8,128)S(1)}, u32[]{:S(2)}) copy-start(f32[1,128,256]{2,1,0:T(8,128)S(1)} %dynamic-slice_bitcast_fusion.4.refs_0_) | copy-start | bytes 393220
  7.3 8.0 %collective-permute-start = (f32[1,128,256]{2,1,0:T(8,128)S(1)}, f32[1,128,256]{2,1,0:T(8,128)S(1)}, u32[]{:S(2)}, u32[]{:S(2)}) collective-permute-start(f32[1,128,256]{2,1,0:T(8,128)S(1)} %dynamic-slice_bitcast_fusion.4.refs_0_), channel_id=1, source_target_pairs={{0,4},{2,6},{1,5},{3,7},{8,12},{10,14},{9,13},{11,15},{16,20},{18,... | collective-permute-start | bytes 393224 | tf_op jit(solution)/shard_map/ppermute | solution.py:329
  11.8 6.9 %collective-permute-start.1 = (f32[1,128,256]{2,1,0:T(8,128)S(1)}, f32[1,128,256]{2,1,0:T(8,128)S(1)}, u32[]{:S(2)}, u32[]{:S(2)}) collective-permute-start(f32[1,128,256]{2,1,0:T(8,128)S(1)} %dynamic-slice_bitcast_fusion.4.refs_0_), channel_id=1, source_target_pairs={{0,2},{2,0},{1,3},{3,1},{8,10},{10,8},{9,11},{11,9},{16,18},{18,16... | collective-permute-start | bytes 393224 | tf_op jit(solution)/shard_map/ppermute | solution.py:333
  15.4 27.9 %copy-start.7 = (f32[1,128,256]{2,1,0:T(8,128)}, f32[1,128,256]{2,1,0:T(8,128)S(1)}, u32[]{:S(2)}) copy-start(f32[1,128,256]{2,1,0:T(8,128)S(1)} %collective-permute-done.refs_2_) | copy-start | bytes 393220
  15.4 3.4 %collective-permute-start.2 = (f32[1,128,256]{2,1,0:T(8,128)S(1)}, f32[1,128,256]{2,1,0:T(8,128)S(1)}, u32[]{:S(2)}, u32[]{:S(2)}) collective-permute-start(f32[1,128,256]{2,1,0:T(8,128)S(1)} %collective-permute-done.refs_2_), channel_id=1, source_target_pairs={{4,6},{6,4},{5,7},{7,5},{12,14},{14,12},{13,15},{15,13},{20,22},{2... | collective-permute-start | bytes 393224 | tf_op jit(solution)/shard_map/ppermute | solution.py:333
  18.7 24.5 %copy-start.8 = (f32[1,128,256]{2,1,0:T(8,128)}, f32[1,128,256]{2,1,0:T(8,128)S(1)}, u32[]{:S(2)}) copy-start(f32[1,128,256]{2,1,0:T(8,128)S(1)} %collective-permute-done.1.refs_1_) | copy-start | bytes 393220
  18.7 1.1 copy-start.9
  23.2 72.3 %copy-start.4 = (f32[6,128,256]{2,1,0:T(8,128)}, f32[6,128,256]{2,1,0:T(8,128)S(1)}, u32[]{:S(2)}) copy-start(f32[6,128,256]{2,1,0:T(8,128)S(1)} %broadcast_select_fusion.2.refs_0_) | copy-start | bytes 2359300
  23.3 9.1 %collective-permute-start.4 = (f32[2,128,256]{2,1,0:T(8,128)S(1)}, f32[2,128,256]{2,1,0:T(8,128)S(1)}, u32[]{:S(2)}, u32[]{:S(2)}) collective-permute-start(f32[2,128,256]{2,1,0:T(8,128)S(1)} %pad_maximum_fusion), channel_id=1, source_target_pairs={{0,16},{8,24},{1,17},{9,25},{2,18},{10,26},{3,19},{11,27},{4,20},{... | collective-permute-start | bytes 786440 | tf_op jit(solution)/shard_map/ppermute | solution.py:361
  32.4 31.1 %collective-permute-start.13 = (f32[6,128,256]{2,1,0:T(8,128)S(1)}, f32[6,128,256]{2,1,0:T(8,128)S(1)}, u32[]{:S(2)}, u32[]{:S(2)}) collective-permute-start(f32[6,128,256]{2,1,0:T(8,128)S(1)} %get-tuple-element.41), channel_id=1, source_target_pairs={{0,16},{8,24},{1,17},{9,25},{2,18},{10,26},{3,19},{11,27},{4,20},{... | collective-permute-start | bytes 2359304 | tf_op jit(solution)/shard_map/ppermute | solution.py:361
  36.8 6.4 %collective-permute-start.5 = (f32[2,128,256]{2,1,0:T(8,128)S(1)}, f32[2,128,256]{2,1,0:T(8,128)S(1)}, u32[]{:S(2)}, u32[]{:S(2)}) collective-permute-start(f32[2,128,256]{2,1,0:T(8,128)S(1)} %broadcast_select_fusion.4.mine), channel_id=1, source_target_pairs={{0,8},{8,0},{16,24},{24,16},{1,9},{9,1},{17,25},{25,17},{2,10},{10... | collective-permute-start | bytes 786440 | tf_op jit(solution)/shard_map/ppermute | solution.py:368
  38.4 13.7 %collective-permute-start.6 = (f32[2,128,256]{2,1,0:T(8,128)S(1)}, f32[2,128,256]{2,1,0:T(8,128)S(1)}, u32[]{:S(2)}, u32[]{:S(2)}) collective-permute-start(f32[2,128,256]{2,1,0:T(8,128)S(1)} %broadcast_select_fusion.4.mine), channel_id=1, source_target_pairs={{0,1},{1,0},{2,3},{3,2},{4,5},{5,4},{6,7},{7,6},{8,9},{9,8},{10,11... | collective-permute-start | bytes 786440 | tf_op jit(solution)/shard_map/ppermute | solution.py:372
  43.2 8.9 %collective-permute-start.7 = (f32[2,128,256]{2,1,0:T(8,128)S(1)}, f32[2,128,256]{2,1,0:T(8,128)S(1)}, u32[]{:S(2)}, u32[]{:S(2)}) collective-permute-start(f32[2,128,256]{2,1,0:T(8,128)S(1)} %collective-permute-done.5.across), channel_id=1, source_target_pairs={{0,1},{1,0},{2,3},{3,2},{4,5},{5,4},{6,7},{7,6},{8,9},{9,8},{10,11... | collective-permute-start | bytes 786440 | tf_op jit(solution)/shard_map/ppermute | solution.py:372
  43.3 52.2 %copy-start.1 = (s32[3]{0:T(128)}, s32[3]{0:T(128)S(1)}, u32[]{:S(2)}) copy-start(s32[3]{0:T(128)S(1)} %pad_add_fusion.place) | copy-start | bytes 40
  44.6 43.7 %collective-permute-start.8 = (f32[7,128,256]{2,1,0:T(8,128)S(1)}, f32[7,128,256]{2,1,0:T(8,128)S(1)}, u32[]{:S(2)}, u32[]{:S(2)}) collective-permute-start(f32[7,128,256]{2,1,0:T(8,128)S(1)} %dynamic-slice_bitcast_fusion), channel_id=1, source_target_pairs={{0,6},{2,4},{1,7},{3,5},{8,14},{10,12},{9,15},{11,13},{16,22},{18,... | collective-permute-start | bytes 2752520 | tf_op jit(solution)/shard_map/ppermute | solution.py:329
  50.5 26.1 %collective-permute-start.10 = (f32[6,128,256]{2,1,0:T(8,128)S(1)}, f32[6,128,256]{2,1,0:T(8,128)}, u32[]{:S(2)}, u32[]{:S(2)}) collective-permute-start(f32[6,128,256]{2,1,0:T(8,128)S(1)} %broadcast_select_fusion.2.refs_0_), channel_id=1, source_target_pairs={{0,8},{8,0},{16,24},{24,16},{1,9},{9,1},{17,25},{25,17},{2,10},{10... | collective-permute-start | bytes 2359304 | tf_op jit(solution)/shard_map/ppermute | solution.py:368
  58.1 33.5 %collective-permute-start.11 = (f32[6,128,256]{2,1,0:T(8,128)S(1)}, f32[6,128,256]{2,1,0:T(8,128)}, u32[]{:S(2)}, u32[]{:S(2)}) collective-permute-start(f32[6,128,256]{2,1,0:T(8,128)S(1)} %broadcast_select_fusion.2.refs_0_), channel_id=1, source_target_pairs={{0,1},{1,0},{2,3},{3,2},{4,5},{5,4},{6,7},{7,6},{8,9},{9,8},{10,11... | collective-permute-start | bytes 2359304 | tf_op jit(solution)/shard_map/ppermute | solution.py:372
  64.5 22.8 %collective-permute-start.14 = (f32[6,128,256]{2,1,0:T(8,128)}, f32[6,128,256]{2,1,0:T(8,128)}, u32[]{:S(2)}, u32[]{:S(2)}) collective-permute-start(f32[6,128,256]{2,1,0:T(8,128)} %broadcast_select_fusion.1.refs_4_), channel_id=1, source_target_pairs={{0,8},{8,0},{16,24},{24,16},{1,9},{9,1},{17,25},{25,17},{2,10},{10... | collective-permute-start | bytes 2359304 | tf_op jit(solution)/shard_map/ppermute | solution.py:368
  75.4 1.0 copy-start
  76.4 19.1 %collective-permute-start.15 = (f32[6,128,256]{2,1,0:T(8,128)}, f32[6,128,256]{2,1,0:T(8,128)}, u32[]{:S(2)}, u32[]{:S(2)}) collective-permute-start(f32[6,128,256]{2,1,0:T(8,128)} %broadcast_select_fusion.1.refs_4_), channel_id=1, source_target_pairs={{0,1},{1,0},{2,3},{3,2},{4,5},{5,4},{6,7},{7,6},{8,9},{9,8},{10,11... | collective-permute-start | bytes 2359304 | tf_op jit(solution)/shard_map/ppermute | solution.py:372
  76.6 18.9 %collective-permute-start.12 = (f32[6,128,256]{2,1,0:T(8,128)}, f32[6,128,256]{2,1,0:T(8,128)}, u32[]{:S(2)}, u32[]{:S(2)}) collective-permute-start(f32[6,128,256]{2,1,0:T(8,128)} %collective-permute-done.10.refs_1_), channel_id=1, source_target_pairs={{0,1},{1,0},{2,3},{3,2},{4,5},{5,4},{6,7},{7,6},{8,9},{9,8},{10,11... | collective-permute-start | bytes 2359304 | tf_op jit(solution)/shard_map/ppermute | solution.py:372
  87.2 8.3 %collective-permute-start.16 = (f32[6,128,256]{2,1,0:T(8,128)}, f32[6,128,256]{2,1,0:T(8,128)}, u32[]{:S(2)}, u32[]{:S(2)}) collective-permute-start(f32[6,128,256]{2,1,0:T(8,128)} %collective-permute-done.14.refs_5_), channel_id=1, source_target_pairs={{0,1},{1,0},{2,3},{3,2},{4,5},{5,4},{6,7},{7,6},{8,9},{9,8},{10,11... | collective-permute-start | bytes 2359304 | tf_op jit(solution)/shard_map/ppermute | solution.py:372
  89.6 34.3 %copy-start.3 = (f32[7,128,256]{2,1,0:T(8,128)}, f32[7,128,256]{2,1,0:T(8,128)S(1)}, u32[]{:S(2)}) copy-start(f32[7,128,256]{2,1,0:T(8,128)S(1)} %broadcast_select_fusion.refs_4_) | copy-start | bytes 2752516
  89.7 32.7 %collective-permute-start.17 = (f32[7,128,256]{2,1,0:T(8,128)S(1)}, f32[7,128,256]{2,1,0:T(8,128)S(1)}, u32[]{:S(2)}, u32[]{:S(2)}) collective-permute-start(f32[7,128,256]{2,1,0:T(8,128)S(1)} %broadcast_select_fusion.refs_4_), channel_id=1, source_target_pairs={{0,2},{4,6},{2,0},{6,4},{1,3},{5,7},{3,1},{7,5},{8,10},{12,14},{10... | collective-permute-start | bytes 2752520 | tf_op jit(solution)/shard_map/ppermute | solution.py:333
  91.7 30.7 %collective-permute-start.9 = (f32[4,128,256]{2,1,0:T(8,128)S(1)}, f32[4,128,256]{2,1,0:T(8,128)S(1)}, u32[]{:S(2)}, u32[]{:S(2)}) collective-permute-start(f32[4,128,256]{2,1,0:T(8,128)S(1)} %dynamic-slice_bitcast_fusion.3), channel_id=1, source_target_pairs={{0,4},{2,6},{1,5},{3,7},{8,12},{10,14},{9,13},{11,15},{16,20},{18,... | collective-permute-start | bytes 1572872 | tf_op jit(solution)/shard_map/ppermute | solution.py:329
  122.4 1.6 copy-start.10
  123.8 20.9 %copy-start.2 = (f32[4,128,256]{2,1,0:T(8,128)}, f32[4,128,256]{2,1,0:T(8,128)S(1)}, u32[]{:S(2)}) copy-start(f32[4,128,256]{2,1,0:T(8,128)S(1)} %broadcast_select_fusion.3.refs_0_) | copy-start | bytes 1572868
  123.8 20.9 %collective-permute-start.18 = (f32[4,128,256]{2,1,0:T(8,128)S(1)}, f32[4,128,256]{2,1,0:T(8,128)S(1)}, u32[]{:S(2)}, u32[]{:S(2)}) collective-permute-start(f32[4,128,256]{2,1,0:T(8,128)S(1)} %broadcast_select_fusion.3.refs_0_), channel_id=1, source_target_pairs={{0,2},{4,6},{2,0},{6,4},{1,3},{5,7},{3,1},{7,5},{8,10},{12,14},{10... | collective-permute-start | bytes 1572872 | tf_op jit(solution)/shard_map/ppermute | solution.py:333
  144.8 0.8 copy-start.5

commit v3 on v2

--- a/solution.py
+++ b/solution.py
@@ -380,7 +380,7 @@
 
 def piece_sizes(count):
     if count == 12:
-        return [1, 7, 4], [(0, 2), (2, 3)]
+        return [1, 5, 6], [(0, 2), (2, 3)]
     return ([1, count - 1] if count > 1 else [1]), [(0, 2)]
 
 

time: 160 us -> 166 us (1.038)
  waiting for transfers between devices: 39.3 us -> 43 us
  starting transfers between devices: 38.6 us -> 40.7 us
    ppermute x4, starting transfers between devices: 6.22 us -> 10.1 us  [exchange(): return lax.ppermute(value, axis, pairs + [(j, i) for i, j in pairs])]
    ppermute x3, starting transfers between devices: 14.3 us -> 12.5 us  [outward(): lax.ppermute(value, axis, [(0, 3), (1, 2)] if turn else [(0, 2), (1, 3)])]
  transfers between devices with their start and end apart: 19 -> 19, of which waited for: 6 -> 8; matrix products, arithmetic and copies ran while one was open for 4% -> 4% of each run, Pallas kernels for 35% -> 32%
where the time goes in v3:
time: 166 us; the launch traced here: 165 us
  Pallas kernels  69.7 us (42%)
  waiting for transfers between devices  43 us (26%)
  starting transfers between devices  40.7 us (25%)
  local copies, waits for them, and re-layouts  7.58 us (5%)
  other arithmetic  3.8 us (2%)
    pallas_call x2, Pallas kernels, update(): pl.pallas_call(functools.partial(update_kernel, sources=len(cands), plan=...  34.6 us
    ppermute x3, waiting for transfers between devices, cross(): return lax.ppermute(value, 'row', [(i, i ^ 1) for i in range(size)])  16 us
    pallas_call x2, Pallas kernels, factor_next(): pl.pallas_call(functools.partial(eliminate_kernel, start=start, stop=stop...  15.7 us
    ppermute x3, waiting for transfers between devices, outward(): lax.ppermute(value, axis, [(0, 3), (1, 2)] if turn else [(0, 2), (1, 3)])  14.7 us
    ppermute x3, starting transfers between devices, spread(): got = lax.ppermute(held, 'row', pairs)  13.8 us
    pallas_call x1, Pallas kernels, columns(): pl.pallas_call(functools.partial(columns_kernel, parts=parts), out_shape=...  13.4 us
    ppermute x3, starting transfers between devices, outward(): lax.ppermute(value, axis, [(0, 3), (1, 2)] if turn else [(0, 2), (1, 3)])  12.5 us
    ppermute x4, starting transfers between devices, exchange(): return lax.ppermute(value, axis, pairs + [(j, i) for i, j in pairs])  10.1 us
  transfers between devices with their start and end apart: 19, of which 8 were waited for; matrix products, arithmetic and copies ran while one was open for 4% of the time, Pallas kernels for 32%

profile of v3, /device:TPU:0, one launch (start us, length us, event | category | flops | bytes accessed | tf_op | source)
XLA Modules:
  0.0 165.1 jit_solution(9261373589097796975)
XLA Ops:
  0.0 1.5 dynamic-slice_bitcast_fusion
  1.5 4.9 %collective-permute-start.3 = (f32[6,128,256]{2,1,0:T(8,128)S(1)}, f32[6,128,256]{2,1,0:T(8,128)S(1)}, u32[]{:S(2)}, u32[]{:S(2)}) collective-permute-start(f32[6,128,256]{2,1,0:T(8,128)S(1)} %get-tuple-element.50), channel_id=1, source_target_pairs={{0,16},{8,24},{1,17},{9,25},{2,18},{10,26},{3,19},{11,27},{4,20},{... | collective-permute-start | bytes 2359304 | tf_op jit(solution)/shard_map/ppermute | solution.py:361
  6.4 0.9 dynamic-slice_bitcast_fusion.4.refs_0_
  7.3 4.5 %collective-permute-start = (f32[1,128,256]{2,1,0:T(8,128)S(1)}, f32[1,128,256]{2,1,0:T(8,128)S(1)}, u32[]{:S(2)}, u32[]{:S(2)}) collective-permute-start(f32[1,128,256]{2,1,0:T(8,128)S(1)} %dynamic-slice_bitcast_fusion.4.refs_0_), channel_id=1, source_target_pairs={{0,4},{2,6},{1,5},{3,7},{8,12},{10,14},{9,13},{11,15},{16,20},{18,... | collective-permute-start | bytes 393224 | tf_op jit(solution)/shard_map/ppermute | solution.py:329
  11.8 3.5 %collective-permute-start.1 = (f32[1,128,256]{2,1,0:T(8,128)S(1)}, f32[1,128,256]{2,1,0:T(8,128)S(1)}, u32[]{:S(2)}, u32[]{:S(2)}) collective-permute-start(f32[1,128,256]{2,1,0:T(8,128)S(1)} %dynamic-slice_bitcast_fusion.4.refs_0_), channel_id=1, source_target_pairs={{0,2},{2,0},{1,3},{3,1},{8,10},{10,8},{9,11},{11,9},{16,18},{18,16... | collective-permute-start | bytes 393224 | tf_op jit(solution)/shard_map/ppermute | solution.py:333
  15.4 0.7 collective-permute-start.2
  16.1 2.7 %collective-permute-done.1.refs_1_ = f32[1,128,256]{2,1,0:T(8,128)S(1)} collective-permute-done((f32[1,128,256]{2,1,0:T(8,128)S(1)}, f32[1,128,256]{2,1,0:T(8,128)S(1)}, u32[]{:S(2)}, u32[]{:S(2)}) %collective-permute-start.1) | collective-permute-done | bytes 131104 | tf_op jit(solution)/shard_map/ppermute | solution.py:333
  18.7 1.0 select_select_fusion.1
  19.8 3.3 %collective-permute-done.3 = f32[6,128,256]{2,1,0:T(8,128)S(1)} collective-permute-done((f32[6,128,256]{2,1,0:T(8,128)S(1)}, f32[6,128,256]{2,1,0:T(8,128)S(1)}, u32[]{:S(2)}, u32[]{:S(2)}) %collective-permute-start.3) | collective-permute-done | bytes 786464 | tf_op jit(solution)/shard_map/ppermute | solution.py:361
  23.1 0.1 broadcast_select_fusion.2.refs_0_
  23.3 4.4 %collective-permute-start.4 = (f32[2,128,256]{2,1,0:T(8,128)S(1)}, f32[2,128,256]{2,1,0:T(8,128)S(1)}, u32[]{:S(2)}, u32[]{:S(2)}) collective-permute-start(f32[2,128,256]{2,1,0:T(8,128)S(1)} %pad_maximum_fusion), channel_id=1, source_target_pairs={{0,16},{8,24},{1,17},{9,25},{2,18},{10,26},{3,19},{11,27},{4,20},{... | collective-permute-start | bytes 786440 | tf_op jit(solution)/shard_map/ppermute | solution.py:361
  27.7 4.7 %collective-permute-done.4 = f32[2,128,256]{2,1,0:T(8,128)S(1)} collective-permute-done((f32[2,128,256]{2,1,0:T(8,128)S(1)}, f32[2,128,256]{2,1,0:T(8,128)S(1)}, u32[]{:S(2)}, u32[]{:S(2)}) %collective-permute-start.4) | collective-permute-done | bytes 262176 | tf_op jit(solution)/shard_map/ppermute | solution.py:361
  32.4 4.4 %collective-permute-start.13 = (f32[6,128,256]{2,1,0:T(8,128)S(1)}, f32[6,128,256]{2,1,0:T(8,128)S(1)}, u32[]{:S(2)}, u32[]{:S(2)}) collective-permute-start(f32[6,128,256]{2,1,0:T(8,128)S(1)} %get-tuple-element.41), channel_id=1, source_target_pairs={{0,16},{8,24},{1,17},{9,25},{2,18},{10,26},{3,19},{11,27},{4,20},{... | collective-permute-start | bytes 2359304 | tf_op jit(solution)/shard_map/ppermute | solution.py:361
  36.8 1.6 collective-permute-start.5
  38.4 0.0 collective-permute-start.6
  38.4 4.9 %collective-permute-done.5.across = f32[2,128,256]{2,1,0:T(8,128)S(1)} collective-permute-done((f32[2,128,256]{2,1,0:T(8,128)S(1)}, f32[2,128,256]{2,1,0:T(8,128)S(1)}, u32[]{:S(2)}, u32[]{:S(2)}) %collective-permute-start.5) | collective-permute-done | bytes 262176 | tf_op jit(solution)/shard_map/ppermute | solution.py:368
  43.2 0.1 pad_add_fusion.place
  43.3 2.0 %dynamic-slice_bitcast_fusion.3 = f32[5,128,256]{2,1,0:T(8,128)} fusion(f32[12,1,12,1,256,256]{5,4,3,2,1,0:T(8,128)} %refs_4_.1, s32[]{:T(128)S(6)} %select_n.77), kind=kLoop, calls=%fused_computation.3 | loop fusion | bytes 1310724 | tf_op jit(solution)/shard_map/reshape | solution.py:411
  45.3 5.9 %collective-permute-start.8 = (f32[5,128,256]{2,1,0:T(8,128)}, f32[5,128,256]{2,1,0:T(8,128)S(1)}, u32[]{:S(2)}, u32[]{:S(2)}) collective-permute-start(f32[5,128,256]{2,1,0:T(8,128)} %dynamic-slice_bitcast_fusion.3), channel_id=1, source_target_pairs={{0,6},{2,4},{1,7},{3,5},{8,14},{10,12},{9,15},{11,13},{16,22},{18,... | collective-permute-start | bytes 1966088 | tf_op jit(solution)/shard_map/ppermute | solution.py:329
  51.3 1.6 collective-permute-start.10
  52.8 0.0 collective-permute-done.6.mine_other
  52.8 0.0 collective-permute-done.7.across_other
  52.8 6.0 %factor_start.1 = (f32[512,512]{1,0:T(8,128)S(1)}, f32[512,512]{1,0:T(8,128)S(1)}) custom-call(s32[3]{0:T(128)S(1)} %pad_add_fusion.place, f32[2,128,256]{2,1,0:T(8,128)S(1)} %broadcast_select_fusion.4.mine, f32[2,128,256]{2,1,0:T(8,128)S(1)} %collective-permute-done.5.across, f32[2,128,256]{2,1,0:T(8,128)S(1)} %collective-permute-done.6.mine_other, ...), custom_call_target="tpu_custom_call" | custom-call | flops 1 | bytes 1 | tf_op jit(solution)/shard_map/factor_start/pallas_call | solution.py:122
  58.9 0.1 collective-permute-start.11
  59.0 5.2 %factor_next.2 = (f32[512,512]{1,0:T(8,128)S(1)}, f32[512,512]{1,0:T(8,128)S(1)}) custom-call(f32[512,512]{1,0:T(8,128)S(1)} %get-tuple-element.28.matrix_in, f32[512,512]{1,0:T(8,128)S(1)} %get-tuple-element.29.inv_in), custom_call_target="tpu_custom_call" | custom-call | flops 1 | bytes 1 | tf_op jit(solution)/shard_map/factor_next/pallas_call | solution.py:137
  64.2 0.1 broadcast_select_fusion.1.refs_4_
  64.3 0.6 collective-permute-start.14
  64.9 10.4 %factor_next.3 = (f32[512,512]{1,0:T(8,128)}, f32[512,512]{1,0:T(8,128)S(1)}) custom-call(f32[512,512]{1,0:T(8,128)S(1)} %get-tuple-element.30.matrix_in, f32[512,512]{1,0:T(8,128)S(1)} %get-tuple-element.31.inv_in), custom_call_target="tpu_custom_call" | custom-call | flops 10000000000 | bytes 1 | tf_op jit(solution)/shard_map/factor_next/pallas_call | solution.py:137
  75.4 1.0 copy-done
  76.3 0.2 collective-permute-start.15
  76.5 0.0 collective-permute-done.10.refs_1_
  76.6 0.3 collective-permute-start.12
  76.8 11.1 %collective-permute-done.14.refs_5_ = f32[6,128,256]{2,1,0:T(8,128)} collective-permute-done((f32[6,128,256]{2,1,0:T(8,128)S(1)}, f32[6,128,256]{2,1,0:T(8,128)}, u32[]{:S(2)}, u32[]{:S(2)}) %collective-permute-start.14) | collective-permute-done | bytes 786464 | tf_op jit(solution)/shard_map/ppermute | solution.py:368
  88.0 0.0 collective-permute-start.16
  88.0 1.2 dynamic-slice_bitcast_fusion.1
  89.2 0.0 collective-permute-done.8
  89.2 1.2 broadcast_select_fusion.3.refs_4_
  90.4 0.1 collective-permute-start.17
  90.5 2.1 %collective-permute-start.9 = (f32[6,128,256]{2,1,0:T(8,128)S(1)}, f32[6,128,256]{2,1,0:T(8,128)S(1)}, u32[]{:S(2)}, u32[]{:S(2)}) collective-permute-start(f32[6,128,256]{2,1,0:T(8,128)S(1)} %dynamic-slice_bitcast_fusion.1), channel_id=1, source_target_pairs={{0,4},{2,6},{1,5},{3,7},{8,12},{10,14},{9,13},{11,15},{16,20},{18,... | collective-permute-start | bytes 2359304 | tf_op jit(solution)/shard_map/ppermute | solution.py:329
  92.7 13.4 %columns.1 = (bf16[1024,3072]{1,0:T(8,128)(2,1)}, f32[8,3072]{1,0:T(8,128)}) custom-call(s32[3]{0:T(128)} %copy-done.1, f32[512,512]{1,0:T(8,128)} %copy-done, f32[6,128,256]{2,1,0:T(8,128)} %copy-done.5, f32[6,128,256]{2,1,0:T(8,128)} %collective-permute-done.10.refs_1_, f32[6,128,256]{2,1,0:T(8,128)} %collective-permute-done.11.refs_2_, ...), custom_call_target="tpu_custom_call" | custom-call | flops 10000000000 | bytes 1 | tf_op jit(solution)/shard_map/columns/pallas_call | solution.py:189
  106.1 1.5 collective-permute-done.17.refs_5_
  107.6 14.7 %collective-permute-done.9 = f32[6,128,256]{2,1,0:T(8,128)S(1)} collective-permute-done((f32[6,128,256]{2,1,0:T(8,128)S(1)}, f32[6,128,256]{2,1,0:T(8,128)S(1)}, u32[]{:S(2)}, u32[]{:S(2)}) %collective-permute-start.9) | collective-permute-done | bytes 786464 | tf_op jit(solution)/shard_map/ppermute | solution.py:329
  122.3 1.2 broadcast_select_fusion.refs_0_
  123.6 5.9 %collective-permute-start.18 = (f32[6,128,256]{2,1,0:T(8,128)S(1)}, f32[6,128,256]{2,1,0:T(8,128)S(1)}, u32[]{:S(2)}, u32[]{:S(2)}) collective-permute-start(f32[6,128,256]{2,1,0:T(8,128)S(1)} %broadcast_select_fusion.refs_0_), channel_id=1, source_target_pairs={{0,2},{4,6},{2,0},{6,4},{1,3},{5,7},{3,1},{7,5},{8,10},{12,14},{10... | collective-permute-start | bytes 2359304 | tf_op jit(solution)/shard_map/ppermute | solution.py:333
  129.4 17.3 %update.2.refs_5_ = f32[12,1,12,1,128,256]{5,4,3,2,1,0:T(8,128)} custom-call(s32[3]{0:T(128)} %copy-done.1, f32[512,512]{1,0:T(8,128)} %copy-done, f32[1,128,256]{2,1,0:T(8,128)} %copy-done.8, f32[1,128,256]{2,1,0:T(8,128)} %copy-done.10, f32[1,128,256]{2,1,0:T(8,128)} %copy-done.9, f32[1,128,256]{2,1,0:T(8,128)} %copy-done.11, f32[5,128,256]{2,1,0:T(8,128)} %copy-done.3, ...), custom_call_target="tpu_custom_call" | custom-call | flops 14495514624 | bytes 18874368 | tf_op jit(solution)/shard_map/update/pallas_call | solution.py:295
  146.8 0.1 collective-permute-done.18.refs_1_
  146.9 1.0 copy-done.4
  147.8 17.3 %update.3 = f32[12,1,12,1,128,256]{5,4,3,2,1,0:T(8,128)} custom-call(s32[3]{0:T(128)} %copy-done.1, f32[512,512]{1,0:T(8,128)} %copy-done, f32[6,128,256]{2,1,0:T(8,128)} %copy-done.2, f32[6,128,256]{2,1,0:T(8,128)} %copy-done.4, bf16[1024,3072]{1,0:T(8,128)(2,1)} %get-tuple-element.47.refs_6_.refs_2_, ...), custom_call_target="tpu_custom_call", output_to_operand_aliasing={{}: (7, {})} | custom-call | flops 14495514624 | bytes 18874368 | tf_op jit(solution)/shard_map/update/pallas_call | solution.py:295
  (32 shorter events, 0.1 us)
Async XLA Ops:
  1.5 21.7 %collective-permute-start.3 = (f32[6,128,256]{2,1,0:T(8,128)S(1)}, f32[6,128,256]{2,1,0:T(8,128)S(1)}, u32[]{:S(2)}, u32[]{:S(2)}) collective-permute-start(f32[6,128,256]{2,1,0:T(8,128)S(1)} %get-tuple-element.50), channel_id=1, source_target_pairs={{0,16},{8,24},{1,17},{9,25},{2,18},{10,26},{3,19},{11,27},{4,20},{... | collective-permute-start | bytes 2359304 | tf_op jit(solution)/shard_map/ppermute | solution.py:361
  7.3 98.7 %copy-start.8 = (f32[1,128,256]{2,1,0:T(8,128)}, f32[1,128,256]{2,1,0:T(8,128)S(1)}, u32[]{:S(2)}) copy-start(f32[1,128,256]{2,1,0:T(8,128)S(1)} %dynamic-slice_bitcast_fusion.4.refs_0_) | copy-start | bytes 393220
  7.3 8.0 %collective-permute-start = (f32[1,128,256]{2,1,0:T(8,128)S(1)}, f32[1,128,256]{2,1,0:T(8,128)S(1)}, u32[]{:S(2)}, u32[]{:S(2)}) collective-permute-start(f32[1,128,256]{2,1,0:T(8,128)S(1)} %dynamic-slice_bitcast_fusion.4.refs_0_), channel_id=1, source_target_pairs={{0,4},{2,6},{1,5},{3,7},{8,12},{10,14},{9,13},{11,15},{16,20},{18,... | collective-permute-start | bytes 393224 | tf_op jit(solution)/shard_map/ppermute | solution.py:329
  11.8 6.9 %collective-permute-start.1 = (f32[1,128,256]{2,1,0:T(8,128)S(1)}, f32[1,128,256]{2,1,0:T(8,128)S(1)}, u32[]{:S(2)}, u32[]{:S(2)}) collective-permute-start(f32[1,128,256]{2,1,0:T(8,128)S(1)} %dynamic-slice_bitcast_fusion.4.refs_0_), channel_id=1, source_target_pairs={{0,2},{2,0},{1,3},{3,1},{8,10},{10,8},{9,11},{11,9},{16,18},{18,16... | collective-permute-start | bytes 393224 | tf_op jit(solution)/shard_map/ppermute | solution.py:333
  15.4 90.7 %copy-start.9 = (f32[1,128,256]{2,1,0:T(8,128)}, f32[1,128,256]{2,1,0:T(8,128)S(1)}, u32[]{:S(2)}) copy-start(f32[1,128,256]{2,1,0:T(8,128)S(1)} %collective-permute-done.refs_2_) | copy-start | bytes 393220
  15.4 3.4 %collective-permute-start.2 = (f32[1,128,256]{2,1,0:T(8,128)S(1)}, f32[1,128,256]{2,1,0:T(8,128)S(1)}, u32[]{:S(2)}, u32[]{:S(2)}) collective-permute-start(f32[1,128,256]{2,1,0:T(8,128)S(1)} %collective-permute-done.refs_2_), channel_id=1, source_target_pairs={{4,6},{6,4},{5,7},{7,5},{12,14},{14,12},{13,15},{15,13},{20,22},{2... | collective-permute-start | bytes 393224 | tf_op jit(solution)/shard_map/ppermute | solution.py:333
  18.7 87.3 %copy-start.10 = (f32[1,128,256]{2,1,0:T(8,128)}, f32[1,128,256]{2,1,0:T(8,128)S(1)}, u32[]{:S(2)}) copy-start(f32[1,128,256]{2,1,0:T(8,128)S(1)} %collective-permute-done.1.refs_1_) | copy-start | bytes 393220
  18.7 1.1 copy-start.11
  23.2 69.4 %copy-start.5 = (f32[6,128,256]{2,1,0:T(8,128)}, f32[6,128,256]{2,1,0:T(8,128)S(1)}, u32[]{:S(2)}) copy-start(f32[6,128,256]{2,1,0:T(8,128)S(1)} %broadcast_select_fusion.2.refs_0_) | copy-start | bytes 2359300
  23.3 9.1 %collective-permute-start.4 = (f32[2,128,256]{2,1,0:T(8,128)S(1)}, f32[2,128,256]{2,1,0:T(8,128)S(1)}, u32[]{:S(2)}, u32[]{:S(2)}) collective-permute-start(f32[2,128,256]{2,1,0:T(8,128)S(1)} %pad_maximum_fusion), channel_id=1, source_target_pairs={{0,16},{8,24},{1,17},{9,25},{2,18},{10,26},{3,19},{11,27},{4,20},{... | collective-permute-start | bytes 786440 | tf_op jit(solution)/shard_map/ppermute | solution.py:361
  32.4 31.8 %collective-permute-start.13 = (f32[6,128,256]{2,1,0:T(8,128)S(1)}, f32[6,128,256]{2,1,0:T(8,128)S(1)}, u32[]{:S(2)}, u32[]{:S(2)}) collective-permute-start(f32[6,128,256]{2,1,0:T(8,128)S(1)} %get-tuple-element.41), channel_id=1, source_target_pairs={{0,16},{8,24},{1,17},{9,25},{2,18},{10,26},{3,19},{11,27},{4,20},{... | collective-permute-start | bytes 2359304 | tf_op jit(solution)/shard_map/ppermute | solution.py:361
  36.8 6.4 %collective-permute-start.5 = (f32[2,128,256]{2,1,0:T(8,128)S(1)}, f32[2,128,256]{2,1,0:T(8,128)S(1)}, u32[]{:S(2)}, u32[]{:S(2)}) collective-permute-start(f32[2,128,256]{2,1,0:T(8,128)S(1)} %broadcast_select_fusion.4.mine), channel_id=1, source_target_pairs={{0,8},{8,0},{16,24},{24,16},{1,9},{9,1},{17,25},{25,17},{2,10},{10... | collective-permute-start | bytes 786440 | tf_op jit(solution)/shard_map/ppermute | solution.py:368
  38.4 14.5 %collective-permute-start.6 = (f32[2,128,256]{2,1,0:T(8,128)S(1)}, f32[2,128,256]{2,1,0:T(8,128)S(1)}, u32[]{:S(2)}, u32[]{:S(2)}) collective-permute-start(f32[2,128,256]{2,1,0:T(8,128)S(1)} %broadcast_select_fusion.4.mine), channel_id=1, source_target_pairs={{0,1},{1,0},{2,3},{3,2},{4,5},{5,4},{6,7},{7,6},{8,9},{9,8},{10,11... | collective-permute-start | bytes 786440 | tf_op jit(solution)/shard_map/ppermute | solution.py:372
  43.2 9.6 %collective-permute-start.7 = (f32[2,128,256]{2,1,0:T(8,128)S(1)}, f32[2,128,256]{2,1,0:T(8,128)S(1)}, u32[]{:S(2)}, u32[]{:S(2)}) collective-permute-start(f32[2,128,256]{2,1,0:T(8,128)S(1)} %collective-permute-done.5.across), channel_id=1, source_target_pairs={{0,1},{1,0},{2,3},{3,2},{4,5},{5,4},{6,7},{7,6},{8,9},{9,8},{10,11... | collective-permute-start | bytes 786440 | tf_op jit(solution)/shard_map/ppermute | solution.py:372
  43.3 49.3 %copy-start.1 = (s32[3]{0:T(128)}, s32[3]{0:T(128)S(1)}, u32[]{:S(2)}) copy-start(s32[3]{0:T(128)S(1)} %pad_add_fusion.place) | copy-start | bytes 40
  45.3 43.8 %collective-permute-start.8 = (f32[5,128,256]{2,1,0:T(8,128)}, f32[5,128,256]{2,1,0:T(8,128)S(1)}, u32[]{:S(2)}, u32[]{:S(2)}) collective-permute-start(f32[5,128,256]{2,1,0:T(8,128)} %dynamic-slice_bitcast_fusion.3), channel_id=1, source_target_pairs={{0,6},{2,4},{1,7},{3,5},{8,14},{10,12},{9,15},{11,13},{16,22},{18,... | collective-permute-start | bytes 1966088 | tf_op jit(solution)/shard_map/ppermute | solution.py:329
  51.3 25.3 %collective-permute-start.10 = (f32[6,128,256]{2,1,0:T(8,128)S(1)}, f32[6,128,256]{2,1,0:T(8,128)}, u32[]{:S(2)}, u32[]{:S(2)}) collective-permute-start(f32[6,128,256]{2,1,0:T(8,128)S(1)} %broadcast_select_fusion.2.refs_0_), channel_id=1, source_target_pairs={{0,8},{8,0},{16,24},{24,16},{1,9},{9,1},{17,25},{25,17},{2,10},{10... | collective-permute-start | bytes 2359304 | tf_op jit(solution)/shard_map/ppermute | solution.py:368
  58.9 31.6 %collective-permute-start.11 = (f32[6,128,256]{2,1,0:T(8,128)S(1)}, f32[6,128,256]{2,1,0:T(8,128)}, u32[]{:S(2)}, u32[]{:S(2)}) collective-permute-start(f32[6,128,256]{2,1,0:T(8,128)S(1)} %broadcast_select_fusion.2.refs_0_), channel_id=1, source_target_pairs={{0,1},{1,0},{2,3},{3,2},{4,5},{5,4},{6,7},{7,6},{8,9},{9,8},{10,11... | collective-permute-start | bytes 2359304 | tf_op jit(solution)/shard_map/ppermute | solution.py:372
  64.3 28.3 %copy-start.6 = (f32[6,128,256]{2,1,0:T(8,128)}, f32[6,128,256]{2,1,0:T(8,128)S(1)}, u32[]{:S(2)}) copy-start(f32[6,128,256]{2,1,0:T(8,128)S(1)} %broadcast_select_fusion.1.refs_4_) | copy-start | bytes 2359300
  64.3 23.6 %collective-permute-start.14 = (f32[6,128,256]{2,1,0:T(8,128)S(1)}, f32[6,128,256]{2,1,0:T(8,128)}, u32[]{:S(2)}, u32[]{:S(2)}) collective-permute-start(f32[6,128,256]{2,1,0:T(8,128)S(1)} %broadcast_select_fusion.1.refs_4_), channel_id=1, source_target_pairs={{0,8},{8,0},{16,24},{24,16},{1,9},{9,1},{17,25},{25,17},{2,10},{10... | collective-permute-start | bytes 2359304 | tf_op jit(solution)/shard_map/ppermute | solution.py:368
  75.4 1.0 copy-start
  76.3 16.3 %collective-permute-start.15 = (f32[6,128,256]{2,1,0:T(8,128)S(1)}, f32[6,128,256]{2,1,0:T(8,128)}, u32[]{:S(2)}, u32[]{:S(2)}) collective-permute-start(f32[6,128,256]{2,1,0:T(8,128)S(1)} %broadcast_select_fusion.1.refs_4_), channel_id=1, source_target_pairs={{0,1},{1,0},{2,3},{3,2},{4,5},{5,4},{6,7},{7,6},{8,9},{9,8},{10,11... | collective-permute-start | bytes 2359304 | tf_op jit(solution)/shard_map/ppermute | solution.py:372
  76.6 16.1 %collective-permute-start.12 = (f32[6,128,256]{2,1,0:T(8,128)}, f32[6,128,256]{2,1,0:T(8,128)}, u32[]{:S(2)}, u32[]{:S(2)}) collective-permute-start(f32[6,128,256]{2,1,0:T(8,128)} %collective-permute-done.10.refs_1_), channel_id=1, source_target_pairs={{0,1},{1,0},{2,3},{3,2},{4,5},{5,4},{6,7},{7,6},{8,9},{9,8},{10,11... | collective-permute-start | bytes 2359304 | tf_op jit(solution)/shard_map/ppermute | solution.py:372
  88.0 4.7 %collective-permute-start.16 = (f32[6,128,256]{2,1,0:T(8,128)}, f32[6,128,256]{2,1,0:T(8,128)}, u32[]{:S(2)}, u32[]{:S(2)}) collective-permute-start(f32[6,128,256]{2,1,0:T(8,128)} %collective-permute-done.14.refs_5_), channel_id=1, source_target_pairs={{0,1},{1,0},{2,3},{3,2},{4,5},{5,4},{6,7},{7,6},{8,9},{9,8},{10,11... | collective-permute-start | bytes 2359304 | tf_op jit(solution)/shard_map/ppermute | solution.py:372
  90.4 39.1 %copy-start.3 = (f32[5,128,256]{2,1,0:T(8,128)}, f32[5,128,256]{2,1,0:T(8,128)S(1)}, u32[]{:S(2)}) copy-start(f32[5,128,256]{2,1,0:T(8,128)S(1)} %broadcast_select_fusion.3.refs_4_) | copy-start | bytes 1966084
  90.4 17.2 %collective-permute-start.17 = (f32[5,128,256]{2,1,0:T(8,128)S(1)}, f32[5,128,256]{2,1,0:T(8,128)S(1)}, u32[]{:S(2)}, u32[]{:S(2)}) collective-permute-start(f32[5,128,256]{2,1,0:T(8,128)S(1)} %broadcast_select_fusion.3.refs_4_), channel_id=1, source_target_pairs={{0,2},{4,6},{2,0},{6,4},{1,3},{5,7},{3,1},{7,5},{8,10},{12,14},{10... | collective-permute-start | bytes 1966088 | tf_op jit(solution)/shard_map/ppermute | solution.py:333
  90.5 31.8 %collective-permute-start.9 = (f32[6,128,256]{2,1,0:T(8,128)S(1)}, f32[6,128,256]{2,1,0:T(8,128)S(1)}, u32[]{:S(2)}, u32[]{:S(2)}) collective-permute-start(f32[6,128,256]{2,1,0:T(8,128)S(1)} %dynamic-slice_bitcast_fusion.1), channel_id=1, source_target_pairs={{0,4},{2,6},{1,5},{3,7},{8,12},{10,14},{9,13},{11,15},{16,20},{18,... | collective-permute-start | bytes 2359304 | tf_op jit(solution)/shard_map/ppermute | solution.py:329
  107.6 21.8 %copy-start.7 = (f32[5,128,256]{2,1,0:T(8,128)}, f32[5,128,256]{2,1,0:T(8,128)S(1)}, u32[]{:S(2)}) copy-start(f32[5,128,256]{2,1,0:T(8,128)S(1)} %collective-permute-done.17.refs_5_) | copy-start | bytes 1966084
  123.5 23.3 %copy-start.2 = (f32[6,128,256]{2,1,0:T(8,128)}, f32[6,128,256]{2,1,0:T(8,128)S(1)}, u32[]{:S(2)}) copy-start(f32[6,128,256]{2,1,0:T(8,128)S(1)} %broadcast_select_fusion.refs_0_) | copy-start | bytes 2359300
  123.6 23.3 %collective-permute-start.18 = (f32[6,128,256]{2,1,0:T(8,128)S(1)}, f32[6,128,256]{2,1,0:T(8,128)S(1)}, u32[]{:S(2)}, u32[]{:S(2)}) collective-permute-start(f32[6,128,256]{2,1,0:T(8,128)S(1)} %broadcast_select_fusion.refs_0_), channel_id=1, source_target_pairs={{0,2},{4,6},{2,0},{6,4},{1,3},{5,7},{3,1},{7,5},{8,10},{12,14},{10... | collective-permute-start | bytes 2359304 | tf_op jit(solution)/shard_map/ppermute | solution.py:333
  146.9 1.0 copy-start.4
